TPU v7x, 32 devices: a whole 2x2x4 slice. The times are simulated.
32 devices in a mesh: dp: 8 (over z, y), grp: 4 (over x, core).
Axes of the slice: x: 2, y: 2, z: 4, core: 2. Of those that a mesh axis runs over, the one named last changes fastest.
Arguments:
- features: bfloat16 [4096, 512], P(('dp', 'grp'))
- loss_scale: bfloat16 [4096], P(('dp', 'grp')), may hold values from 8 to 32
- blocks: int32 [4096, 8], P(('dp', 'grp')), may hold values from 0 to 31, all different within a row; in each aligned block of 128 rows (0 to 127, 128 to 255, ...) at most 48 rows name the same one
- label_col: int32 [4096], P(('dp', 'grp')), may hold values from 0 to 1023
- block_slot: int32 [32], replicated, may hold values from 0 to 31, each once
- centers: bfloat16 [32768, 512], P(('dp', 'grp'))
Outputs:
- loss_out: float32 [4096], P(('dp', 'grp'))
- feature_grad: float32 [4096, 512], P(('dp', 'grp'))
- center_grad: bfloat16 [32768, 512], P(('dp', 'grp'))
Inputs may be any that keep to these rules, and one draw needn't show every extreme that they name: Each row names 8 different blocks; the first is the sample's own block. Among the rows of one device no block is named by more than 48 rows, and some block is named by exactly 48. A permutation: block b is stored in rows block_slot[b] * 1024 to block_slot[b] * 1024 + 1023 of centers.
All inputs are finite; a program needn't handle non-finite values.
Results may differ from a plain program's by a relative error of at most 0.0054.
Values may be sent and summed in bfloat16 or wider, within the bound.
A program may use at most 64 MiB of HBM per device.

v0:
```python
import jax
import jax.numpy as jnp
from jax import lax
from jax.sharding import PartitionSpec as P

BLOCK = 1024


MARGIN = 0.35
LOGIT_SCALE = 64.0
EPSILON = 1e-06


def normalize(block_w):
    widened = block_w.astype(jnp.float32)
    lengths = jnp.sqrt(jnp.sum(widened * widened, axis=1) + EPSILON)
    unit_rows = widened / lengths[:, None]
    return (unit_rows.astype(jnp.bfloat16), unit_rows, lengths)


def normalize_block(block_w):
    squares = jnp.einsum("re,re->r", block_w, block_w, preferred_element_type=jnp.float32)
    lengths = jnp.sqrt(squares + EPSILON)
    unit_rows = block_w.astype(jnp.float32) / lengths[:, None]
    scaled = unit_rows.astype(jnp.bfloat16) * LOGIT_SCALE
    return (scaled, unit_rows, lengths)


def block_logits(rows_x, scaled_centers, columns):
    width = scaled_centers.shape[0]
    scores = lax.dot_general(
        rows_x, scaled_centers, (((1,), (1,)), ((), ())), preferred_element_type=jnp.float32
    )
    row_iota = jnp.arange(rows_x.shape[0], dtype=jnp.int32)
    target_cols = jnp.where(columns >= 0, columns, width)
    scores = scores.at[row_iota, target_cols].add(-LOGIT_SCALE * MARGIN, mode="drop")
    picked = jnp.where(columns >= 0, scores[row_iota, jnp.maximum(columns, 0)], 0.0)
    return (scores, picked)


def center_terms(exps, factor, columns, gains, rows_x, scaled_centers, unit_rows, lengths):
    width = scaled_centers.shape[0]
    row_iota = jnp.arange(exps.shape[0], dtype=jnp.int32)
    target_cols = jnp.where(columns >= 0, columns, width)
    weights = exps * factor[:, None]
    weights = (
        weights.at[row_iota, target_cols]
        .add(-gains.astype(jnp.float32), mode="drop")
        .astype(jnp.bfloat16)
    )
    returned = jnp.dot(weights, scaled_centers, preferred_element_type=jnp.float32)
    scaled_rows = rows_x * LOGIT_SCALE
    unit_grad = lax.dot_general(
        weights, scaled_rows, (((0,), (0,)), ((), ())), preferred_element_type=jnp.float32
    )
    along_unit = jnp.einsum("re,re->r", unit_rows, unit_grad)
    grad_rows = ((unit_grad - unit_rows * along_unit[:, None]) / lengths[:, None]).astype(
        jnp.bfloat16
    )
    return (returned, grad_rows)


def route_rows(rows_out, gains_out, sample_tags, col_tags):
    return (
        lax.all_to_all(
            lax.all_to_all(rows_out, "dp", split_axis=2, concat_axis=2, tiled=True),
            "grp",
            split_axis=1,
            concat_axis=1,
            tiled=True,
        ),
        lax.all_to_all(
            lax.all_to_all(gains_out, "dp", split_axis=2, concat_axis=2, tiled=True),
            "grp",
            split_axis=1,
            concat_axis=1,
            tiled=True,
        ),
        lax.all_to_all(
            lax.all_to_all(sample_tags, "dp", split_axis=2, concat_axis=2, tiled=True),
            "grp",
            split_axis=1,
            concat_axis=1,
            tiled=True,
        ),
        lax.all_to_all(
            lax.all_to_all(col_tags, "dp", split_axis=2, concat_axis=2, tiled=True),
            "grp",
            split_axis=1,
            concat_axis=1,
            tiled=True,
        ),
    )


def route_grads(returned):
    return lax.all_to_all(
        lax.all_to_all(returned, "dp", split_axis=2, concat_axis=2, tiled=True),
        "grp",
        split_axis=1,
        concat_axis=1,
        tiled=True,
    )


def on_device(features, loss_scale, blocks, label_col, block_slot, centers):
    dp_count = lax.axis_size("dp")
    groups = lax.axis_size("grp")
    sample_count, feature_width = features.shape
    pick_count = blocks.shape[1]
    block_total = block_slot.shape[0]
    per_device = centers.shape[0] // BLOCK
    quota = (sample_count * pick_count + block_total - 1) // block_total
    capacity_most = quota + max(1, quota // 2)
    pair_count = sample_count * pick_count
    layout = (per_device, groups, dp_count, capacity_most)
    slot_total = per_device * groups * dp_count * capacity_most
    capacity = groups * dp_count * capacity_most
    normed_feat, unit_feat, feat_norm = normalize(features)
    flat_blocks = blocks.reshape(-1)
    matches = flat_blocks[:, None] == lax.broadcasted_iota(jnp.int32, (pair_count, block_total), 1)
    slot_ids = jnp.sum(jnp.where(matches, block_slot[None, :], 0), axis=1)
    owner_flat = slot_ids // per_device
    local_block = slot_ids % per_device
    owner_grp = owner_flat % groups
    owner_dp = owner_flat // groups
    sample_of = lax.broadcasted_iota(jnp.int32, (sample_count, pick_count), 0).reshape(-1)
    pick_of = lax.broadcasted_iota(jnp.int32, (sample_count, pick_count), 1).reshape(-1)
    earlier = (flat_blocks[:, None] == flat_blocks[None, :]) & (
        sample_of[None, :] < sample_of[:, None]
    )
    rank_of = jnp.sum(earlier.astype(jnp.int32), axis=1)
    places = ((local_block * groups + owner_grp) * dp_count + owner_dp) * capacity_most + rank_of
    rows_out = (
        jnp.zeros((slot_total, feature_width), jnp.bfloat16)
        .at[places]
        .set(jnp.repeat(normed_feat, pick_count, axis=0))
    )
    gains_out = (
        jnp.zeros((slot_total,), jnp.bfloat16).at[places].set(jnp.repeat(loss_scale, pick_count))
    )
    sample_tags = jnp.full((slot_total,), -1, jnp.int32).at[places].set(sample_of)
    col_values = jnp.where(pick_of == 0, jnp.repeat(label_col, pick_count), -1)
    col_tags = jnp.full((slot_total,), -1, jnp.int32).at[places].set(col_values)
    rows_in, gains_in, samples_in, cols_in = route_rows(
        rows_out.reshape(layout + (feature_width,)),
        gains_out.reshape(layout),
        sample_tags.reshape(layout),
        col_tags.reshape(layout),
    )
    local_idx = 0
    scaled_centers, unit_rows, lengths = normalize_block(centers)
    rows_x = rows_in[local_idx].reshape(capacity, feature_width)
    columns = cols_in[local_idx].reshape(capacity)
    scores, picked = block_logits(rows_x, scaled_centers, columns)
    tag_rows = samples_in[local_idx].reshape(capacity)
    gains = gains_in[local_idx].reshape(capacity)
    local_data = [
        (scores, picked, rows_x, scaled_centers, unit_rows, lengths, gains, tag_rows, columns)
    ]
    entry = local_data[0]
    highest = jnp.max(entry[0], axis=1)
    exps = jnp.exp(entry[0] - highest[:, None])
    exps_list = [exps]
    highs = [highest]
    totals = [jnp.sum(exps, axis=1)]
    picks_list = [entry[1]]
    back_high, back_total, back_pick = (
        lax.all_to_all(
            lax.all_to_all(
                jnp.stack(highs).reshape(layout), "dp", split_axis=2, concat_axis=2, tiled=True
            ),
            "grp",
            split_axis=1,
            concat_axis=1,
            tiled=True,
        ),
        lax.all_to_all(
            lax.all_to_all(
                jnp.stack(totals).reshape(layout), "dp", split_axis=2, concat_axis=2, tiled=True
            ),
            "grp",
            split_axis=1,
            concat_axis=1,
            tiled=True,
        ),
        lax.all_to_all(
            lax.all_to_all(
                jnp.stack(picks_list).reshape(layout), "dp", split_axis=2, concat_axis=2, tiled=True
            ),
            "grp",
            split_axis=1,
            concat_axis=1,
            tiled=True,
        ),
    )
    pair_high = back_high.reshape(-1)[places].reshape(sample_count, pick_count)
    pair_total = back_total.reshape(-1)[places].reshape(sample_count, pick_count)
    pair_pick = back_pick.reshape(-1)[places].reshape(sample_count, pick_count)
    sample_peak = jnp.max(pair_high, axis=1)
    sample_denom = jnp.sum(pair_total * jnp.exp(pair_high - sample_peak[:, None]), axis=1)
    target = jnp.sum(pair_pick, axis=1)
    peak_out = (
        jnp.zeros((slot_total,), jnp.float32).at[places].set(jnp.repeat(sample_peak, pick_count))
    )
    denom_out = (
        jnp.ones((slot_total,), jnp.float32).at[places].set(jnp.repeat(sample_denom, pick_count))
    )
    peak_in, denom_in = (
        lax.all_to_all(
            lax.all_to_all(peak_out.reshape(layout), "dp", split_axis=2, concat_axis=2, tiled=True),
            "grp",
            split_axis=1,
            concat_axis=1,
            tiled=True,
        ),
        lax.all_to_all(
            lax.all_to_all(
                denom_out.reshape(layout), "dp", split_axis=2, concat_axis=2, tiled=True
            ),
            "grp",
            split_axis=1,
            concat_axis=1,
            tiled=True,
        ),
    )
    local_idx = 0
    row_peak = peak_in[local_idx].reshape(capacity)
    row_denom = denom_in[local_idx].reshape(capacity)
    gains = local_data[local_idx][6].astype(jnp.float32)
    factors = [gains * jnp.exp(highs[local_idx] - row_peak) / row_denom]
    loss_out = sample_peak + jnp.log(sample_denom) - target
    local_idx = 0
    entry = local_data[local_idx]
    returned, grad_rows = center_terms(
        exps_list[local_idx],
        factors[local_idx],
        entry[8],
        entry[6],
        entry[2],
        entry[3],
        entry[4],
        entry[5],
    )
    returned_list = [returned]
    back_grads = route_grads(jnp.stack(returned_list).reshape(layout + (feature_width,)))
    pair_grads = back_grads.reshape(slot_total, feature_width)[places].reshape(
        sample_count, pick_count, feature_width
    )
    unit_fgrad = jnp.sum(pair_grads, axis=1)
    along = jnp.sum(unit_feat * unit_fgrad, axis=1, keepdims=True)
    feature_grad = (unit_fgrad - unit_feat * along) / feat_norm[:, None]
    return (loss_out, feature_grad, grad_rows)


def solution(mesh):
    placed = (
        P(("dp", "grp"), None),
        P(("dp", "grp")),
        P(("dp", "grp"), None),
        P(("dp", "grp")),
        P(),
        P(("dp", "grp"), None),
    )
    return jax.shard_map(
        on_device,
        mesh=mesh,
        in_specs=placed,
        out_specs=(P(("dp", "grp")), P(("dp", "grp"), None), P(("dp", "grp"), None)),
        check_vma=False,
    )
```

profile of v0, /device:TPU:0, one launch (start us, length us, event | category | flops | bytes accessed | tf_op | source)
XLA Modules:
  0.0 417.7 jit_solution(6505545568737330011)
XLA Ops:
  4.3 4.3 %scatter_custom_fusion.1 = s32[1536]{0:T(1024)S(1)} fusion(s32[1024]{0:T(1024)S(1)} %bitcast.136, s32[1024]{0:T(1024)S(1)} %reshape.308, s32[]{:T(128)} %constant.71.clone.1), kind=kCustom, calls=%fused_computation.63 | custom fusion | bytes 6148 | tf_op jit(solution)/shard_map/scatter | solution.py:144
  9.4 7.3 %all-to-all-start.2 = ((s32[8,1,192]{2,1,0:T(1,128)}), s32[8,1,192]{2,1,0:T(1,128)S(1)}, u32[]{:S(2)}, u32[]{:S(2)}) async-start(s32[8,1,192]{2,1,0:T(1,128)} %reshape.364), calls=%async_computation.2 | async-start | bytes 16384 | tf_op jit(solution)/shard_map/all_to_all | solution.py:87
  18.7 5.6 %scatter_custom_fusion = bf16[1536,512]{1,0:T(8,128)(2,1)S(1)} fusion(s32[1024]{0:T(1024)S(1)} %bitcast.137, bf16[]{:T(256)} %constant.64.clone.1, bf16[128,512]{1,0:T(8,128)(2,1)S(1)} %fusion.25), kind=kCustom, calls=%fused_computation.25 | custom fusion | bytes 1703938 | tf_op jit(solution)/shard_map/scatter | solution.py:137
  25.6 6.0 %all-to-all-start = ((bf16[1,4,8,48,512]{4,3,1,0,2:T(8,128)(2,1)}), bf16[1,4,8,48,512]{4,3,1,0,2:T(8,128)(2,1)S(1)}, u32[]{:S(2)}, u32[]{:S(2)}) async-start(bf16[1,4,8,48,512]{4,3,1,0,2:T(8,128)(2,1)} %copy.42), calls=%async_computation | async-start | bytes 3145728 | tf_op jit(solution)/shard_map/all_to_all | solution.py:66
  33.5 34.5 %all-to-all-done = bf16[1,4,8,48,512]{4,3,1,0,2:T(8,128)(2,1)S(1)} async-done(((bf16[1,4,8,48,512]{4,3,1,0,2:T(8,128)(2,1)}), bf16[1,4,8,48,512]{4,3,1,0,2:T(8,128)(2,1)S(1)}, u32[]{:S(2)}, u32[]{:S(2)}) %all-to-all-start) | async-done | bytes 1572896 | tf_op jit(solution)/shard_map/all_to_all | solution.py:66
  78.8 7.6 %scatter_custom_fusion.2 = bf16[1536]{0:T(1024)(128)(2,1)S(1)} fusion(s32[1024]{0:T(1024)S(1)} %bitcast.138, bf16[1024]{0:T(1024)(128)(2,1)S(1)} %reshape.316, bf16[]{:T(256)} %constant.64.clone.1), kind=kCustom, calls=%fused_computation.67 | custom fusion | bytes 3074 | tf_op jit(solution)/shard_map/scatter | solution.py:140
  88.5 10.1 %all-to-all-done.1 = bf16[1,4,8,48,512]{4,3,2,0,1:T(8,128)(2,1)S(1)} async-done(((bf16[1,4,8,48,512]{4,3,2,0,1:T(8,128)(2,1)}), bf16[1,4,8,48,512]{4,3,2,0,1:T(8,128)(2,1)S(1)}, u32[]{:S(2)}, u32[]{:S(2)}) %all-to-all-start.1) | async-done | bytes 1572896 | tf_op jit(solution)/shard_map/all_to_all | solution.py:65
  104.3 4.2 %copy.68 = f32[192,8,8,128]{3,1,2,0:T(8,128)} copy(f32[192,8,8,128]{3,2,1,0:T(8,128)S(1)} %convolution_bitcast_fusion) | data formatting | bytes 12582912
  108.5 13.3 %scatter_fusion = f32[1572864]{0:T(1024)} fusion(f32[1572864]{0:T(1024)} %bitcast.104, s32[1536]{0:T(1024)S(1)} %broadcast_select_fusion, f32[1536]{0:T(1024)S(1)} %broadcast.230), kind=kCustom, calls=%fused_computation.10 | custom fusion | flops 1536 | bytes 24576
  121.8 7.1 %reshape.251 = f32[1536,1024]{1,0:T(8,128)} reshape(f32[1572864]{0:T(1024)} %scatter_fusion) | data formatting | bytes 12582912 | tf_op jit(solution)/shard_map/scatter-add | solution.py:36
  132.8 6.0 %all-to-all-start.4 = ((f32[8,1,192]{2,1,0:T(1,128)}), f32[8,1,192]{2,1,0:T(1,128)S(1)}, u32[]{:S(2)}, u32[]{:S(2)}) async-start(f32[8,1,192]{2,1,0:T(1,128)} %reshape.372), calls=%async_computation.4 | async-start | bytes 16384 | tf_op jit(solution)/shard_map/all_to_all | solution.py:170
  138.8 3.9 fusion
  145.3 4.2 %all-to-all-start.6 = ((f32[8,1,192]{2,1,0:T(1,128)}), f32[8,1,192]{2,1,0:T(1,128)S(1)}, u32[]{:S(2)}, u32[]{:S(2)}) async-start(f32[8,1,192]{2,1,0:T(1,128)} %reshape.376), calls=%async_computation.6 | async-start | bytes 16384 | tf_op jit(solution)/shard_map/all_to_all | solution.py:179
  151.4 4.6 %all-to-all-done.6 = f32[8,1,192]{2,1,0:T(1,128)S(1)} async-done(((f32[8,1,192]{2,1,0:T(1,128)}), f32[8,1,192]{2,1,0:T(1,128)S(1)}, u32[]{:S(2)}, u32[]{:S(2)}) %all-to-all-start.6) | async-done | bytes 6176 | tf_op jit(solution)/shard_map/all_to_all | solution.py:179
  167.8 6.2 %gather_fusion = f32[1024]{0:T(1024)S(1)} fusion(f32[1536]{0:T(1024)S(1)} %reshape.234, s32[1024]{0:T(1024)S(1)} %broadcast_clamp_fusion), kind=kCustom, calls=%fused_computation | custom fusion | bytes 12288 | tf_op jit(solution)/shard_map/gather | solution.py:197
  178.3 6.2 %gather_fusion.1 = f32[1024]{0:T(1024)S(1)} fusion(f32[1536]{0:T(1024)S(1)} %reshape.236, s32[1024]{0:T(1024)S(1)} %broadcast_clamp_fusion), kind=kCustom, calls=%fused_computation.1 | custom fusion | bytes 12288 | tf_op jit(solution)/shard_map/gather | solution.py:198
  184.9 4.3 %scatter_custom_fusion.4 = f32[1536]{0:T(1024)S(1)} fusion(s32[1024]{0:T(1024)S(1)} %bitcast.140, f32[1024]{0:T(1024)S(1)} %reshape.332, f32[]{:T(128)} %constant.80.clone.1), kind=kCustom, calls=%fused_computation.58 | custom fusion | bytes 6148 | tf_op jit(solution)/shard_map/scatter | solution.py:207
  193.5 4.3 %scatter_custom_fusion.3 = f32[1536]{0:T(1024)S(1)} fusion(s32[1024]{0:T(1024)S(1)} %bitcast.141, f32[1024]{0:T(1024)S(1)} %reshape.324, f32[]{:T(128)} %constant.74.clone.1), kind=kCustom, calls=%fused_computation.60 | custom fusion | bytes 6148 | tf_op jit(solution)/shard_map/scatter | solution.py:204
  199.8 4.8 %all-to-all-start.12 = ((f32[8,1,192]{2,1,0:T(1,128)}), f32[8,1,192]{2,1,0:T(1,128)S(1)}, u32[]{:S(2)}, u32[]{:S(2)}) async-start(f32[8,1,192]{2,1,0:T(1,128)} %reshape.386), calls=%async_computation.12 | async-start | bytes 16384 | tf_op jit(solution)/shard_map/all_to_all | solution.py:211
  206.0 5.1 %all-to-all-done.12 = f32[8,1,192]{2,1,0:T(1,128)S(1)} async-done(((f32[8,1,192]{2,1,0:T(1,128)}), f32[8,1,192]{2,1,0:T(1,128)S(1)}, u32[]{:S(2)}, u32[]{:S(2)}) %all-to-all-start.12) | async-done | bytes 6176 | tf_op jit(solution)/shard_map/all_to_all | solution.py:211
  214.5 24.1 %gather_fusion.2 = f32[1536]{0:T(1024)S(1)} fusion(f32[1536,1024]{1,0:T(8,128)} %reshape.251, s32[1536]{0:T(1024)S(1)} %get-tuple-element.5), kind=kCustom, calls=%fused_computation.2 | custom fusion | bytes 24576 | tf_op jit(solution)/shard_map/gather | solution.py:37
  240.1 3.8 all-to-all-start.13
  255.6 4.2 %copy.69 = f32[192,8,8,128]{3,1,2,0:T(8,128)} copy(f32[192,8,8,128]{3,2,1,0:T(8,128)S(1)} %multiply_bitcast_fusion) | data formatting | bytes 12582912
  259.8 13.3 %scatter_fusion.1 = f32[1572864]{0:T(1024)} fusion(f32[1572864]{0:T(1024)} %bitcast.103, s32[1536]{0:T(1024)S(1)} %broadcast_select_fusion, f32[1536]{0:T(1024)S(1)} %get-tuple-element.3), kind=kCustom, calls=%fused_computation.11 | custom fusion | flops 1536 | bytes 24576
  279.5 4.1 fusion.9
  285.6 5.9 %all-to-all-start.16 = ((f32[1,4,8,48,512]{4,3,1,0,2:T(8,128)}), f32[1,4,8,48,512]{4,3,1,0,2:T(8,128)S(1)}, u32[]{:S(2)}, u32[]{:S(2)}) async-start(f32[1,4,8,48,512]{4,3,1,0,2:T(8,128)} %copy.58), calls=%async_computation.16 | async-start | bytes 6291456 | tf_op jit(solution)/shard_map/all_to_all | solution.py:98
  293.0 69.0 %all-to-all-done.16 = f32[1,4,8,48,512]{4,3,1,0,2:T(8,128)S(1)} async-done(((f32[1,4,8,48,512]{4,3,1,0,2:T(8,128)}), f32[1,4,8,48,512]{4,3,1,0,2:T(8,128)S(1)}, u32[]{:S(2)}, u32[]{:S(2)}) %all-to-all-start.16) | async-done | bytes 3145760 | tf_op jit(solution)/shard_map/all_to_all | solution.py:98
  369.0 3.7 all-to-all-start.17
  373.5 6.2 %gather_fusion.3 = f32[1024]{0:T(1024)S(1)} fusion(f32[1536]{0:T(1024)S(1)} %reshape.238, s32[1024]{0:T(1024)S(1)} %broadcast_clamp_fusion), kind=kCustom, calls=%fused_computation.3 | custom fusion | bytes 12288 | tf_op jit(solution)/shard_map/gather | solution.py:199
  380.4 4.6 %multiply_reduce_fusion = (f32[1024]{0:T(1024)S(1)}, f32[1024,512]{1,0:T(8,128)S(1)}) fusion(f32[1024]{0:T(1024)S(1)} %add_sqrt_fusion, bf16[1024,512]{1,0:T(8,128)(2,1)} %param.11, bf16[1536,1024]{1,0:T(8,128)(2,1)} %reshape.257, bf16[1536,512]{1,0:T(8,128)(2,1)} %bitcast.108), kind=kOutput, calls=%fused_computation.21 | convolution fusion | flops 1613495296 | bytes 7872512 | tf_op jit(solution)/shard_map/dot_general | solution.py:53
  386.5 23.1 %all-to-all-done.17 = f32[1,4,8,48,512]{4,3,2,0,1:T(8,128)S(1)} async-done(((f32[1,4,8,48,512]{4,3,2,0,1:T(8,128)}), f32[1,4,8,48,512]{4,3,2,0,1:T(8,128)S(1)}, u32[]{:S(2)}, u32[]{:S(2)}) %all-to-all-start.17) | async-done | bytes 3145760 | tf_op jit(solution)/shard_map/all_to_all | solution.py:97
  409.6 4.9 %gather_fusion.4 = f32[1024,512]{1,0:T(8,128)} fusion(f32[1536,512]{1,0:T(8,128)S(1)} %bitcast.102, s32[1024]{0:T(1024)S(1)} %broadcast_clamp_fusion), kind=kCustom, calls=%fused_computation.4 | custom fusion | bytes 4198400 | tf_op jit(solution)/shard_map/gather | solution.py:247
  (153 shorter events, 100.4 us)
Async XLA Ops:
  9.4 16.2 %all-to-all-start.2 = ((s32[8,1,192]{2,1,0:T(1,128)}), s32[8,1,192]{2,1,0:T(1,128)S(1)}, u32[]{:S(2)}, u32[]{:S(2)}) async-start(s32[8,1,192]{2,1,0:T(1,128)} %reshape.364), calls=%async_computation.2 | async-start | bytes 16384 | tf_op jit(solution)/shard_map/all_to_all | solution.py:87
  25.6 42.4 %all-to-all-start = ((bf16[1,4,8,48,512]{4,3,1,0,2:T(8,128)(2,1)}), bf16[1,4,8,48,512]{4,3,1,0,2:T(8,128)(2,1)S(1)}, u32[]{:S(2)}, u32[]{:S(2)}) async-start(bf16[1,4,8,48,512]{4,3,1,0,2:T(8,128)(2,1)} %copy.42), calls=%async_computation | async-start | bytes 3145728 | tf_op jit(solution)/shard_map/all_to_all | solution.py:66
  68.0 7.0 %all-to-all-start.3 = ((s32[4,1,384]{2,1,0:T(1,128)}), s32[4,1,384]{2,1,0:T(1,128)S(1)}, u32[]{:S(2)}, u32[]{:S(2)}) async-start(s32[4,1,384]{2,1,0:T(1,128)} %reshape.366), calls=%async_computation.3 | async-start | bytes 12288 | tf_op jit(solution)/shard_map/all_to_all | solution.py:86
  72.6 6.1 %copy-start.4 = (bf16[128]{0:T(256)(128)(2,1)S(1)}, bf16[128]{0:T(256)(128)(2,1)}, u32[]{:S(2)}) copy-start(bf16[128]{0:T(256)(128)(2,1)} %param.7) | copy-start | bytes 772
  72.6 14.5 %copy-start = (bf16[1024,512]{1,0:T(8,128)(2,1)S(1)}, bf16[1024,512]{1,0:T(8,128)(2,1)}, u32[]{:S(2)}) copy-start(bf16[1024,512]{1,0:T(8,128)(2,1)} %param.11) | copy-start | bytes 3145732
  72.6 15.7 %copy-start.6 = (s32[2]{0:T(128)S(1)}, s32[2]{0:T(128)}, u32[]{:S(2)}) copy-start(s32[2]{0:T(128)} %constant.81) | copy-start | bytes 28
  72.6 15.8 %copy-start.5 = (s32[2]{0:T(128)S(1)}, s32[2]{0:T(128)}, u32[]{:S(2)}) copy-start(s32[2]{0:T(128)} %constant.84) | copy-start | bytes 28
  75.1 23.6 %all-to-all-start.1 = ((bf16[1,4,8,48,512]{4,3,2,0,1:T(8,128)(2,1)}), bf16[1,4,8,48,512]{4,3,2,0,1:T(8,128)(2,1)S(1)}, u32[]{:S(2)}, u32[]{:S(2)}) async-start(bf16[1,4,8,48,512]{4,3,2,0,1:T(8,128)(2,1)} %copy.43), calls=%async_computation.1 | async-start | bytes 3145728 | tf_op jit(solution)/shard_map/all_to_all | solution.py:65
  98.7 5.6 %copy-start.3 = (bf16[1,4,8,48,512]{4,3,2,0,1:T(8,128)(2,1)}, bf16[1,4,8,48,512]{4,3,2,0,1:T(8,128)(2,1)S(1)}, u32[]{:S(2)}) copy-start(bf16[1,4,8,48,512]{4,3,2,0,1:T(8,128)(2,1)S(1)} %all-to-all-done.1) | copy-start | bytes 4718596
  98.7 34.1 %all-to-all-start.10 = ((bf16[1,4,8,48]{3,1,0,2:T(4,128)(2,1)}), bf16[1,4,8,48]{3,1,0,2:T(4,128)(2,1)S(1)}, u32[]{:S(2)}, u32[]{:S(2)}) async-start(bf16[1,4,8,48]{3,1,0,2:T(4,128)(2,1)} %copy.52), calls=%async_computation.10 | async-start | bytes 16384 | tf_op jit(solution)/shard_map/all_to_all | solution.py:73
  132.8 12.5 %all-to-all-start.4 = ((f32[8,1,192]{2,1,0:T(1,128)}), f32[8,1,192]{2,1,0:T(1,128)S(1)}, u32[]{:S(2)}, u32[]{:S(2)}) async-start(f32[8,1,192]{2,1,0:T(1,128)} %reshape.372), calls=%async_computation.4 | async-start | bytes 16384 | tf_op jit(solution)/shard_map/all_to_all | solution.py:170
  145.3 10.7 %all-to-all-start.6 = ((f32[8,1,192]{2,1,0:T(1,128)}), f32[8,1,192]{2,1,0:T(1,128)S(1)}, u32[]{:S(2)}, u32[]{:S(2)}) async-start(f32[8,1,192]{2,1,0:T(1,128)} %reshape.376), calls=%async_computation.6 | async-start | bytes 16384 | tf_op jit(solution)/shard_map/all_to_all | solution.py:179
  156.0 7.0 %all-to-all-start.5 = ((f32[4,1,384]{2,1,0:T(1,128)}), f32[4,1,384]{2,1,0:T(1,128)S(1)}, u32[]{:S(2)}, u32[]{:S(2)}) async-start(f32[4,1,384]{2,1,0:T(1,128)} %reshape.374), calls=%async_computation.5 | async-start | bytes 12288 | tf_op jit(solution)/shard_map/all_to_all | solution.py:169
  163.0 11.2 %all-to-all-start.7 = ((f32[4,1,384]{2,1,0:T(1,128)}), f32[4,1,384]{2,1,0:T(1,128)S(1)}, u32[]{:S(2)}, u32[]{:S(2)}) async-start(f32[4,1,384]{2,1,0:T(1,128)} %reshape.378), calls=%async_computation.7 | async-start | bytes 12288 | tf_op jit(solution)/shard_map/all_to_all | solution.py:178
  174.2 15.8 %all-to-all-start.11 = ((bf16[4,2,192]{2,1,0:T(2,128)(2,1)}), bf16[4,2,192]{2,1,0:T(2,128)(2,1)S(1)}, u32[]{:S(2)}, u32[]{:S(2)}) async-start(bf16[4,2,192]{2,1,0:T(2,128)(2,1)} %reshape.384), calls=%async_computation.11 | async-start | bytes 8192 | tf_op jit(solution)/shard_map/all_to_all | solution.py:72
  190.0 9.8 %all-to-all-start.14 = ((f32[8,1,192]{2,1,0:T(1,128)}), f32[8,1,192]{2,1,0:T(1,128)S(1)}, u32[]{:S(2)}, u32[]{:S(2)}) async-start(f32[8,1,192]{2,1,0:T(1,128)} %reshape.380), calls=%async_computation.14 | async-start | bytes 16384 | tf_op jit(solution)/shard_map/all_to_all | solution.py:218
  199.8 11.3 %all-to-all-start.12 = ((f32[8,1,192]{2,1,0:T(1,128)}), f32[8,1,192]{2,1,0:T(1,128)S(1)}, u32[]{:S(2)}, u32[]{:S(2)}) async-start(f32[8,1,192]{2,1,0:T(1,128)} %reshape.386), calls=%async_computation.12 | async-start | bytes 16384 | tf_op jit(solution)/shard_map/all_to_all | solution.py:211
  211.1 29.1 %all-to-all-start.15 = ((f32[4,1,384]{2,1,0:T(1,128)}), f32[4,1,384]{2,1,0:T(1,128)S(1)}, u32[]{:S(2)}, u32[]{:S(2)}) async-start(f32[4,1,384]{2,1,0:T(1,128)} %reshape.382), calls=%async_computation.15 | async-start | bytes 12288 | tf_op jit(solution)/shard_map/all_to_all | solution.py:217
  240.1 7.6 %all-to-all-start.13 = ((f32[4,1,384]{2,1,0:T(1,128)}), f32[4,1,384]{2,1,0:T(1,128)S(1)}, u32[]{:S(2)}, u32[]{:S(2)}) async-start(f32[4,1,384]{2,1,0:T(1,128)} %reshape.388), calls=%async_computation.13 | async-start | bytes 12288 | tf_op jit(solution)/shard_map/all_to_all | solution.py:210
  247.7 37.9 %all-to-all-start.8 = ((f32[8,1,192]{2,1,0:T(1,128)}), f32[8,1,192]{2,1,0:T(1,128)S(1)}, u32[]{:S(2)}, u32[]{:S(2)}) async-start(f32[8,1,192]{2,1,0:T(1,128)} %reshape.368), calls=%async_computation.8 | async-start | bytes 16384 | tf_op jit(solution)/shard_map/all_to_all | solution.py:188
  285.6 76.3 %all-to-all-start.16 = ((f32[1,4,8,48,512]{4,3,1,0,2:T(8,128)}), f32[1,4,8,48,512]{4,3,1,0,2:T(8,128)S(1)}, u32[]{:S(2)}, u32[]{:S(2)}) async-start(f32[1,4,8,48,512]{4,3,1,0,2:T(8,128)} %copy.58), calls=%async_computation.16 | async-start | bytes 6291456 | tf_op jit(solution)/shard_map/all_to_all | solution.py:98
  361.9 7.0 %all-to-all-start.9 = ((f32[4,1,384]{2,1,0:T(1,128)}), f32[4,1,384]{2,1,0:T(1,128)S(1)}, u32[]{:S(2)}, u32[]{:S(2)}) async-start(f32[4,1,384]{2,1,0:T(1,128)} %reshape.370), calls=%async_computation.9 | async-start | bytes 12288 | tf_op jit(solution)/shard_map/all_to_all | solution.py:187
  369.0 40.6 %all-to-all-start.17 = ((f32[1,4,8,48,512]{4,3,2,0,1:T(8,128)}), f32[1,4,8,48,512]{4,3,2,0,1:T(8,128)S(1)}, u32[]{:S(2)}, u32[]{:S(2)}) async-start(f32[1,4,8,48,512]{4,3,2,0,1:T(8,128)} %copy.59), calls=%async_computation.17 | async-start | bytes 6291456 | tf_op jit(solution)/shard_map/all_to_all | solution.py:97
  380.4 4.6 %copy-start.1 = (bf16[1024,512]{1,0:T(8,128)(2,1)S(1)}, bf16[1024,512]{1,0:T(8,128)(2,1)}, u32[]{:S(2)}) copy-start(bf16[1024,512]{1,0:T(8,128)(2,1)} %param.11) | copy-start | bytes 3145732
  414.4 2.2 copy-start.2
where the time goes:
time: 420 us; the launch traced here: 418 us
  waiting for transfers between devices  158 us (38%)
  local copies, waits for them, and re-layouts  114 us (27%)
  starting transfers between devices  75.3 us (18%)
  other arithmetic  59 us (14%)
  matrix products  10.6 us (3%)
    all_to_all x1, waiting for transfers between devices, route_grads(): lax.all_to_all(returned, 'dp', split_axis=2, concat_axis=2, tiled=True)  69 us
    all_to_all x1, waiting for transfers between devices, route_rows(): lax.all_to_all(rows_out, 'dp', split_axis=2, concat_axis=2, tiled=True)  34.5 us
    unnamed x6, other arithmetic  30.3 us
    gather x2, local copies, waits for them, and re-layouts, block_logits(): scores[row_iota, jnp.maximum(columns, 0)]  24.1 us
    all_to_all x1, waiting for transfers between devices, route_grads(): lax.all_to_all(lax.all_to_all(returned, 'dp', split_axis=2, concat_axis=2...  23.1 us
    unnamed x44, local copies, waits for them, and re-layouts  19.2 us
    all_to_all x1, waiting for transfers between devices, route_rows(): lax.all_to_all(lax.all_to_all(rows_out, 'dp', split_axis=2, concat_axis=2...  10.1 us
  transfers between devices with their start and end apart: 18, of which 12 were waited for; matrix products, arithmetic and copies ran while one was open for 40% of the time, Pallas kernels for 0%

commit v1 on v0

--- a/solution.py
+++ b/solution.py
@@ -1,6 +1,10 @@
+import functools
+
 import jax
 import jax.numpy as jnp
 from jax import lax
+from jax.experimental import pallas as pl
+from jax.experimental.pallas import tpu as pltpu
 from jax.sharding import PartitionSpec as P
 
 BLOCK = 1024
@@ -253,6 +257,639 @@
     return (loss_out, feature_grad, grad_rows)
 
 
+MESH = pl.DeviceIdType.MESH
+VMEM = pl.BlockSpec(memory_space=pltpu.VMEM)
+SMEM = pl.BlockSpec(memory_space=pltpu.SMEM)
+TAG_ROWS = 16
+SPLIT = 32
+VMEM_LIMIT = 56 * 1024 * 1024
+
+
+class Place:
+    def __init__(self, depth):
+        dp, grp = lax.axis_index("dp"), lax.axis_index("grp")
+        self.depth = depth
+        self.z, y = lax.div(dp, 2), lax.rem(dp, 2)
+        x, self.c = lax.div(grp, 2), lax.rem(grp, 2)
+        self.a = y + self.c * (x - y)
+        self.b = x + self.c * (y - x)
+        self.me = dp * 4 + grp
+
+    def device(self, z, a, b, c):
+        y, x = a + c * (b - a), b + c * (a - b)
+        return (z * 2 + y, x * 2 + c)
+
+    def origin(self, z, a, b, c):
+        dp, grp = self.device(z, a, b, c)
+        return dp * 4 + grp
+
+    def up(self):
+        return self.device(self.z + 1, self.a, self.b, self.c)
+
+    def down(self):
+        return self.device(self.z - 1, self.a, self.b, self.c)
+
+    def first(self):
+        return self.device(self.z, 1 - self.a, self.b, self.c)
+
+    def second(self):
+        return self.device(self.z, self.a, 1 - self.b, self.c)
+
+    def sibling(self):
+        return self.device(self.z, self.b, self.a, 1 - self.c)
+
+    def inside(self, offset):
+        if offset == 0:
+            return None
+        return self.z + offset < self.depth if offset > 0 else self.z + offset >= 0
+
+    def when(self, offset, body):
+        if offset == 0:
+            body()
+        else:
+            pl.when(self.inside(offset))(body)
+
+
+def offsets_at(distance):
+    return [0] if distance == 0 else [-distance, distance]
+
+
+def greet(place):
+    barrier = pltpu.get_barrier_semaphore()
+    for target in (place.sibling(), place.first(), place.second()):
+        pl.semaphore_signal(barrier, inc=1, device_id=target, device_id_type=MESH)
+
+    @pl.when(place.z > 0)
+    def _():
+        pl.semaphore_signal(barrier, inc=1, device_id=place.down(), device_id_type=MESH)
+
+    @pl.when(place.z < place.depth - 1)
+    def _():
+        pl.semaphore_signal(barrier, inc=1, device_id=place.up(), device_id_type=MESH)
+
+    last = place.depth - 1
+    below, above = lax.div(place.z + last, place.depth), lax.div(2 * last - place.z, place.depth)
+    pl.semaphore_wait(barrier, 3 + below + above)
+
+
+UP, DOWN, FIRST, SECOND, SIB = range(5)
+
+
+def gather_kernel(depth, x_ref, tags_ref, g_ref, send, recv):
+    place = Place(depth)
+    rows = x_ref.shape[0]
+    widened = x_ref[...].astype(jnp.float32)
+    lengths = jnp.sqrt(jnp.sum(widened * widened, axis=1, keepdims=True) + EPSILON)
+    g_ref[place.me, 0:rows, :] = (widened / lengths).astype(jnp.bfloat16)
+    g_ref[place.me, rows : rows + TAG_ROWS, :] = tags_ref[...]
+    greet(place)
+
+    def copy(slot, way, target):
+        return pltpu.make_async_remote_copy(
+            src_ref=g_ref.at[slot],
+            dst_ref=g_ref.at[slot],
+            send_sem=send.at[way, slot],
+            recv_sem=recv.at[slot],
+            device_id=target,
+            device_id_type=MESH,
+        )
+
+    def arrived(slot):
+        copy(slot, SIB, place.sibling()).wait_recv()
+
+    z, a, b, c = place.z, place.a, place.b, place.c
+
+    def along_z(offset, act):
+        slot = place.origin(z + offset, a, b, c)
+        if offset <= 0:
+            pl.when(z < depth - 1)(lambda: act(copy(slot, UP, place.up())))
+        if offset >= 0:
+            pl.when(z > 0)(lambda: act(copy(slot, DOWN, place.down())))
+
+    def spread(slot, ways, act):
+        if FIRST in ways:
+            act(copy(slot, FIRST, place.first()))
+        if SECOND in ways:
+            act(copy(slot, SECOND, place.second()))
+        act(copy(slot, SIB, place.sibling()))
+
+    def events():
+        for r in range(depth + 2):
+            if r < depth:
+                for off in offsets_at(r):
+                    yield off, 0
+            if 1 <= r <= depth:
+                for off in offsets_at(r - 1):
+                    yield off, 1
+                    yield off, 2
+            if 2 <= r <= depth + 1:
+                for off in offsets_at(r - 2):
+                    yield off, 3
+
+    def handle(off, kind, act, wait):
+        def body():
+            slot = place.origin(
+                z + off, 1 - a if kind & 1 else a, 1 - b if kind & 2 else b, c
+            )
+            if wait and (off != 0 or kind != 0):
+                arrived(slot)
+            if kind == 0:
+                along_z(off, act)
+            spread(slot, ((FIRST, SECOND), (SECOND,), (), ())[kind], act)
+
+        place.when(off, body)
+
+    for off, kind in events():
+        handle(off, kind, lambda item: item.start(), True)
+    for off, kind in events():
+
+        def other():
+            arrived(
+                place.origin(
+                    z + off, 1 - b if kind & 1 else b, 1 - a if kind & 2 else a, 1 - c
+                )
+            )
+
+        place.when(off, other)
+    for off, kind in events():
+        handle(off, kind, lambda item: item.wait_send(), False)
+
+
+def gather_rows(depth, devices, features, tags):
+    rows, width = features.shape
+    return pl.pallas_call(
+        functools.partial(gather_kernel, depth),
+        out_shape=jax.ShapeDtypeStruct((devices, rows + TAG_ROWS, width), jnp.bfloat16),
+        in_specs=[VMEM, VMEM],
+        out_specs=VMEM,
+        scratch_shapes=[
+            pltpu.SemaphoreType.DMA((5, devices)),
+            pltpu.SemaphoreType.DMA((devices,)),
+        ],
+        compiler_params=pltpu.CompilerParams(
+            collective_id=0, has_side_effects=True, vmem_limit_bytes=VMEM_LIMIT
+        ),
+        name="gather_rows",
+    )(features, tags)
+
+
+def chosen(rank_ref, o, most):
+    rank = rank_ref[pl.ds(o, 1), :]
+    shape = (most, rank.shape[1])
+    return lax.broadcasted_iota(jnp.int32, shape, 0).astype(jnp.float32) == rank
+
+
+def center_parts(c_ref):
+    widened = c_ref[...].astype(jnp.float32)
+    lengths = jnp.sqrt(jnp.sum(widened * widened, axis=1, keepdims=True) + EPSILON)
+    return widened / lengths, lengths
+
+
+def scores_kernel(
+    most, block_ref, g_ref, c_ref, xc_ref, e_ref, part_ref, pick_ref, rank_ref, gain_ref, colc_ref, cn_ref, col_ref, sum_ref, tgt_ref
+):
+    devices, rows = g_ref.shape[0], g_ref.shape[1] - TAG_ROWS
+    width = c_ref.shape[0]
+    mine = block_ref[0].astype(jnp.float32)
+    cn_ref[...] = (center_parts(c_ref)[0].astype(jnp.bfloat16) * LOGIT_SCALE).astype(jnp.bfloat16)
+    tags = g_ref[:, rows : rows + TAG_ROWS, 0:rows].astype(jnp.float32)
+    place = lax.broadcasted_iota(jnp.int32, tags.shape, 1)
+    hit = tags == mine
+
+    def row(n):
+        return jnp.sum(jnp.where(place == n, tags, 0.0), axis=1)
+
+    named = jnp.sum(jnp.where(hit & (place < 8), 1.0, 0.0), axis=1)
+    own = jnp.sum(jnp.where(hit & (place == 0), 1.0, 0.0), axis=1)
+    earlier = lax.broadcasted_iota(jnp.int32, (rows, rows), 0) < lax.broadcasted_iota(jnp.int32, (rows, rows), 1)
+    ahead = jnp.dot(
+        named.astype(jnp.bfloat16),
+        jnp.where(earlier, 1.0, 0.0).astype(jnp.bfloat16),
+        preferred_element_type=jnp.float32,
+    )
+    rank_ref[...] = jnp.where(named > 0.0, ahead, -1.0)
+    gain_ref[...] = row(10)
+    col_ref[...] = jnp.where(own > 0.0, row(8) * SPLIT + row(9) + 1.0, 0.0)
+
+    @pl.loop(0, devices, unroll=4)
+    def _(o):
+        pick = chosen(rank_ref, o, most)
+        at = pl.ds(pl.multiple_of(o * most, 16), most)
+        xc_ref[at, :] = jnp.dot(
+            jnp.where(pick, 1.0, 0.0).astype(jnp.bfloat16), g_ref[o, 0:rows, :], preferred_element_type=jnp.float32
+        ).astype(jnp.bfloat16)
+        colc_ref[at, :] = jnp.sum(jnp.where(pick, col_ref[pl.ds(o, 1), :], 0.0), axis=1, keepdims=True) - 1.0
+
+    step = 8 * most
+
+    @pl.loop(0, devices * most // step)
+    def _(i):
+        at = pl.ds(pl.multiple_of(i * step, 16), step)
+        scores = lax.dot_general(
+            xc_ref[at, :], cn_ref[...], (((1,), (1,)), ((), ())), preferred_element_type=jnp.float32
+        )
+        positive = lax.broadcasted_iota(jnp.int32, scores.shape, 1).astype(jnp.float32) == colc_ref[at, :]
+        scores = scores - jnp.where(positive, LOGIT_SCALE * MARGIN, 0.0)
+        exps = jnp.exp(scores)
+        e_ref[at, :] = exps
+        sum_ref[at, :] = jnp.sum(exps, axis=1, keepdims=True)
+        tgt_ref[at, :] = jnp.sum(jnp.where(positive, scores, 0.0), axis=1, keepdims=True)
+
+    @pl.loop(0, devices, unroll=4)
+    def _(o):
+        pick = chosen(rank_ref, o, most)
+        at = pl.ds(pl.multiple_of(o * most, 16), most)
+        part_ref[pl.ds(o, 1), :] = jnp.sum(jnp.where(pick, sum_ref[at, :], 0.0), axis=0, keepdims=True)
+        pick_ref[pl.ds(o, 1), :] = jnp.sum(jnp.where(pick, tgt_ref[at, :], 0.0), axis=0, keepdims=True)
+
+
+def block_scores(most, block, gathered, centers):
+    devices, rows, width = gathered.shape
+    rows = rows - TAG_ROWS
+    capacity = devices * most
+    f32 = jnp.float32
+    return pl.pallas_call(
+        functools.partial(scores_kernel, most),
+        out_shape=(
+            jax.ShapeDtypeStruct((capacity, width), jnp.bfloat16),
+            jax.ShapeDtypeStruct((capacity, centers.shape[0]), f32),
+            jax.ShapeDtypeStruct((devices, rows), f32),
+            jax.ShapeDtypeStruct((devices, rows), f32),
+            jax.ShapeDtypeStruct((devices, rows), f32),
+            jax.ShapeDtypeStruct((devices, rows), f32),
+            jax.ShapeDtypeStruct((capacity, 1), f32),
+        ),
+        in_specs=[SMEM, VMEM, VMEM],
+        out_specs=(VMEM,) * 7,
+        scratch_shapes=[
+            pltpu.VMEM(centers.shape, jnp.bfloat16),
+            pltpu.VMEM((devices, rows), f32),
+            pltpu.VMEM((capacity, 1), f32),
+            pltpu.VMEM((capacity, 1), f32),
+        ],
+        compiler_params=pltpu.CompilerParams(vmem_limit_bytes=VMEM_LIMIT),
+        name="block_scores",
+    )(block, gathered, centers)
+
+
+def totals_kernel(depth, part_ref, pick_ref, total_ref, loss_ref, held, landed, send, recv):
+    place = Place(depth)
+    devices = part_ref.shape[0]
+    held[0, 0:devices, :] = part_ref[...]
+    held[0, devices : 2 * devices, :] = pick_ref[...]
+    barrier = pltpu.get_barrier_semaphore()
+    others = [place.sibling(), place.first(), place.second()]
+    turns = [
+        place.device(lax.rem(place.z + k, depth), place.a, place.b, place.c) for k in range(1, depth)
+    ]
+    for target in others + turns:
+        pl.semaphore_signal(barrier, inc=1, device_id=target, device_id_type=MESH)
+    pl.semaphore_wait(barrier, len(others) + len(turns))
+
+    def copy(n, at, target):
+        return pltpu.make_async_remote_copy(
+            src_ref=held.at[at],
+            dst_ref=landed.at[n],
+            send_sem=send.at[n],
+            recv_sem=recv.at[n],
+            device_id=target,
+            device_id_type=MESH,
+        )
+
+    copies = []
+    for n, target in enumerate(others):
+        item = copy(n, n, target)
+        item.start()
+        copies.append(item)
+        item.wait_recv()
+        held[n + 1] = held[n] + landed[n]
+    last = len(others)
+    for k, target in enumerate(turns):
+        item = copy(last + k, last, target)
+        item.start()
+        copies.append(item)
+    total = held[last]
+    for k in range(len(turns)):
+        copies[last + k].wait_recv()
+        total = total + landed[last + k]
+    total_ref[...] = total[0:devices]
+    held[last + 1] = total
+    mine = pl.ds(place.me, 1)
+    loss_ref[...] = jnp.log(held[last + 1, mine, :]) - held[last + 1, pl.ds(place.me + devices, 1), :]
+    for item in copies:
+        item.wait_send()
+
+
+def sample_totals(depth, part, pick):
+    devices, rows = part.shape
+    steps = depth + 2
+    return pl.pallas_call(
+        functools.partial(totals_kernel, depth),
+        out_shape=(
+            jax.ShapeDtypeStruct(part.shape, jnp.float32),
+            jax.ShapeDtypeStruct((1, rows), jnp.float32),
+        ),
+        in_specs=[VMEM, VMEM],
+        out_specs=(VMEM, VMEM),
+        scratch_shapes=[
+            pltpu.VMEM((5, 2 * devices, rows), jnp.float32),
+            pltpu.VMEM((steps, 2 * devices, rows), jnp.float32),
+            pltpu.SemaphoreType.DMA((steps,)),
+            pltpu.SemaphoreType.DMA((steps,)),
+        ],
+        compiler_params=pltpu.CompilerParams(
+            collective_id=1, has_side_effects=True, vmem_limit_bytes=VMEM_LIMIT
+        ),
+        name="sample_totals",
+    )(part, pick)
+
+
+def grads_kernel(most, total_ref, rank_ref, gain_ref, colc_ref, xc_ref, e_ref, c_ref, r_ref, cg_ref, cn_ref, fac_ref, ug_ref, facc_ref, gainc_ref):
+    devices, rows = rank_ref.shape
+    cn_ref[...] = (center_parts(c_ref)[0].astype(jnp.bfloat16) * LOGIT_SCALE).astype(jnp.bfloat16)
+    fac_ref[...] = gain_ref[...] / total_ref[...]
+    ug_ref[...] = jnp.zeros_like(ug_ref)
+
+    @pl.loop(0, devices, unroll=4)
+    def _(o):
+        pick = chosen(rank_ref, o, most)
+        at = pl.ds(pl.multiple_of(o * most, 16), most)
+        facc_ref[at, :] = jnp.sum(jnp.where(pick, fac_ref[pl.ds(o, 1), :], 0.0), axis=1, keepdims=True)
+        gainc_ref[at, :] = jnp.sum(jnp.where(pick, gain_ref[pl.ds(o, 1), :], 0.0), axis=1, keepdims=True)
+
+    group = 8
+    step = group * most
+
+    @pl.loop(0, devices // group)
+    def _(i):
+        at = pl.ds(pl.multiple_of(i * step, 16), step)
+        exps = e_ref[at, :]
+        positive = lax.broadcasted_iota(jnp.int32, exps.shape, 1).astype(jnp.float32) == colc_ref[at, :]
+        weights = exps * facc_ref[at, :] - jnp.where(positive, gainc_ref[at, :], 0.0)
+        weights = weights.astype(jnp.bfloat16)
+        returned = jnp.dot(weights, cn_ref[...], preferred_element_type=jnp.float32).astype(jnp.bfloat16)
+        ug_ref[...] += lax.dot_general(
+            weights, xc_ref[at, :], (((0,), (0,)), ((), ())), preferred_element_type=jnp.float32
+        )
+        for k in range(group):
+            o = i * group + k
+            pick = jnp.where(chosen(rank_ref, o, most), 1.0, 0.0).astype(jnp.bfloat16)
+            r_ref[o] = lax.dot_general(
+                pick,
+                returned[k * most : (k + 1) * most],
+                (((0,), (0,)), ((), ())),
+                preferred_element_type=jnp.float32,
+            ).astype(jnp.bfloat16)
+
+    unit, lengths = center_parts(c_ref)
+    grad = ug_ref[...] * LOGIT_SCALE
+    along = jnp.sum(unit * grad, axis=1, keepdims=True)
+    cg_ref[...] = ((grad - unit * along) / lengths).astype(jnp.bfloat16)
+
+
+def block_grads(most, total, rank, gain, colc, xc, exps, centers):
+    devices, rows = rank.shape
+    capacity, width = xc.shape
+    return pl.pallas_call(
+        functools.partial(grads_kernel, most),
+        out_shape=(
+            jax.ShapeDtypeStruct((devices, rows, width), jnp.bfloat16),
+            jax.ShapeDtypeStruct(centers.shape, jnp.bfloat16),
+        ),
+        in_specs=[VMEM] * 7,
+        out_specs=(VMEM, VMEM),
+        scratch_shapes=[
+            pltpu.VMEM(centers.shape, jnp.bfloat16),
+            pltpu.VMEM((devices, rows), jnp.float32),
+            pltpu.VMEM(centers.shape, jnp.float32),
+            pltpu.VMEM((capacity, 1), jnp.float32),
+            pltpu.VMEM((capacity, 1), jnp.float32),
+        ],
+        compiler_params=pltpu.CompilerParams(vmem_limit_bytes=VMEM_LIMIT),
+        name="block_grads",
+    )(total, rank, gain, colc, xc, exps, centers)
+
+
+def scatter_kernel(depth, r_ref, x_ref, out_ref, rs, tx2, rx2, tx1, rx1, txz, rxu, rxd, s_sib, v_sib, s2, v2, s1, v1, sz, vu, vd):
+    place = Place(depth)
+    z, a, b, c = place.z, place.a, place.b, place.c
+    f32 = jnp.float32
+    greet(place)
+
+    def far_first():
+        for r in range(depth - 1, -1, -1):
+            for off in offsets_at(r):
+                yield off
+
+    def copy(src, dst, send, recv, target):
+        return pltpu.make_async_remote_copy(
+            src_ref=src, dst_ref=dst, send_sem=send, recv_sem=recv, device_id=target, device_id_type=MESH
+        )
+
+    def to_sibling(off, kind):
+        o = place.origin(z + off, 1 - b if kind & 1 else b, 1 - a if kind & 2 else a, 1 - c)
+        h = lax.div(o, 2)
+        return copy(r_ref.at[o], rs.at[h], s_sib.at[h], v_sib.at[h], place.sibling())
+
+    def own_sum(off, kind):
+        o = place.origin(z + off, 1 - a if kind & 1 else a, 1 - b if kind & 2 else b, c)
+        h = lax.div(o, 2)
+        copy(r_ref.at[o], rs.at[h], s_sib.at[h], v_sib.at[h], place.sibling()).wait_recv()
+        return r_ref[o].astype(f32) + rs[h].astype(f32)
+
+    def to_second(off, kind):
+        slot = (z + off) * 2 + (1 - a if kind & 1 else a)
+        return slot, copy(tx2.at[slot], rx2.at[slot], s2.at[slot], v2.at[slot], place.second())
+
+    def to_first(off):
+        slot = z + off
+        return slot, copy(tx1.at[slot], rx1.at[slot], s1.at[slot], v1.at[slot], place.first())
+
+    def to_up(off):
+        slot = z + off
+        return slot, copy(txz.at[slot], rxu.at[slot], sz.at[slot], vu.at[slot], place.up())
+
+    def to_down(off):
+        slot = z + off
+        return slot, copy(txz.at[slot], rxd.at[slot], sz.at[slot], vd.at[slot], place.down())
+
+    order = (3, 2, 1, 0)
+    for kind in order:
+        for off in far_first():
+            place.when(off, lambda: to_sibling(off, kind).start())
+
+    for kind in (3, 2):
+        for off in far_first():
+
+            def cross_second():
+                total = own_sum(off, kind)
+                slot, item = to_second(off, kind)
+                tx2[slot] = total.astype(jnp.bfloat16)
+                item.start()
+
+            place.when(off, cross_second)
+    for off in far_first():
+
+        def cross_first():
+            total = own_sum(off, 1)
+            far, item = to_second(off, 1)
+            item.wait_recv()
+            total = total + rx2[far].astype(f32)
+            slot, item = to_first(off)
+            tx1[slot] = total.astype(jnp.bfloat16)
+            item.start()
+
+        place.when(off, cross_first)
+
+    def gathered_sum(off):
+        total = own_sum(off, 0)
+        far, item = to_second(off, 0)
+        item.wait_recv()
+        total = total + rx2[far].astype(f32)
+        near, item = to_first(off)
+        item.wait_recv()
+        return total + rx1[near].astype(f32)
+
+    for off in far_first():
+        if off == 0:
+            continue
+
+        def cross_z():
+            slot, item = to_up(off) if off > 0 else to_down(off)
+            txz[slot] = gathered_sum(off).astype(jnp.bfloat16)
+
+            @pl.when(z > 0 if off > 0 else z < depth - 1)
+            def _():
+                item.wait_recv()
+                landed = rxu if off > 0 else rxd
+                txz[slot] = (txz[slot].astype(f32) + landed[slot].astype(f32)).astype(jnp.bfloat16)
+
+            item.start()
+
+        place.when(off, cross_z)
+
+    out_ref[...] = gathered_sum(0)
+
+    @pl.when(z > 0)
+    def _():
+        slot, item = to_up(0)
+        item.wait_recv()
+        out_ref[...] += rxu[slot].astype(f32)
+
+    @pl.when(z < depth - 1)
+    def _():
+        slot, item = to_down(0)
+        item.wait_recv()
+        out_ref[...] += rxd[slot].astype(f32)
+
+    widened = x_ref[...].astype(f32)
+    lengths = jnp.sqrt(jnp.sum(widened * widened, axis=1, keepdims=True) + EPSILON)
+    unit = widened / lengths
+    grad = out_ref[...]
+    along = jnp.sum(unit * grad, axis=1, keepdims=True)
+    out_ref[...] = (grad - unit * along) / lengths
+
+    for off in far_first():
+
+        def drain():
+            for kind in order:
+                to_sibling(off, kind).wait_send()
+            for kind in (3, 2):
+                to_second(off, kind)[1].wait_send()
+            to_first(off)[1].wait_send()
+            if off > 0:
+                to_up(off)[1].wait_send()
+            if off < 0:
+                to_down(off)[1].wait_send()
+
+        place.when(off, drain)
+
+
+def scatter_rows(depth, returned, features):
+    devices, rows, width = returned.shape
+
+    def slots(count):
+        return pltpu.VMEM((count, rows, width), jnp.bfloat16)
+
+    def sems(count):
+        return pltpu.SemaphoreType.DMA((count,))
+
+    return pl.pallas_call(
+        functools.partial(scatter_kernel, depth),
+        out_shape=jax.ShapeDtypeStruct((rows, width), jnp.float32),
+        in_specs=[VMEM, VMEM],
+        out_specs=VMEM,
+        scratch_shapes=[
+            slots(devices // 2),
+            slots(depth * 2),
+            slots(depth * 2),
+            slots(depth),
+            slots(depth),
+            slots(depth),
+            slots(depth),
+            slots(depth),
+            sems(devices // 2),
+            sems(devices // 2),
+            sems(depth * 2),
+            sems(depth * 2),
+            sems(depth),
+            sems(depth),
+            sems(depth),
+            sems(depth),
+            sems(depth),
+        ],
+        compiler_params=pltpu.CompilerParams(
+            collective_id=2, has_side_effects=True, vmem_limit_bytes=VMEM_LIMIT
+        ),
+        name="scatter_rows",
+    )(returned, features)
+
+
+def on_device_dense(depth, most, features, loss_scale, blocks, label_col, block_slot, centers):
+    devices = depth * 8
+    rows, width = features.shape
+    me = lax.axis_index("dp") * 4 + lax.axis_index("grp")
+    block = jnp.sum(jnp.where(block_slot == me, jnp.arange(block_slot.shape[0], dtype=jnp.int32), 0)).reshape(1)
+    bf16 = jnp.bfloat16
+    tags = jnp.concatenate(
+        [
+            blocks.T.astype(bf16),
+            (label_col // SPLIT).astype(bf16)[None],
+            (label_col % SPLIT).astype(bf16)[None],
+            loss_scale[None],
+        ]
+    )
+    tags = jnp.pad(tags, ((0, TAG_ROWS - tags.shape[0]), (0, width - rows)))
+    gathered = gather_rows(depth, devices, features, tags)
+    xc, exps, part, pick, rank, gain, colc = block_scores(most, block, gathered, centers)
+    total, loss = sample_totals(depth, part, pick)
+    returned, center_grad = block_grads(most, total, rank, gain, colc, xc, exps, centers)
+    feature_grad = scatter_rows(depth, returned, features)
+    return loss.reshape(-1), feature_grad, center_grad
+
+
+def chosen_plan(mesh, features, loss_scale, blocks, label_col, block_slot, centers):
+    dp_count, groups = mesh.shape["dp"], mesh.shape["grp"]
+    rows, picks = blocks.shape
+    total = block_slot.shape[0]
+    quota = (rows * picks + total - 1) // total
+    most = quota + max(1, quota // 2)
+    dense = (
+        most * 4 >= rows
+        and most % 16 == 0
+        and rows == 128
+        and groups == 4
+        and dp_count % 2 == 0
+        and total == dp_count * groups
+        and total <= 256
+        and picks == 8
+    )
+    args = (features, loss_scale, blocks, label_col, block_slot, centers)
+    if dense:
+        return on_device_dense(dp_count // 2, most, *args)
+    return on_device(*args)
+
+
 def solution(mesh):
     placed = (
         P(("dp", "grp"), None),
@@ -263,7 +900,7 @@
         P(("dp", "grp"), None),
     )
     return jax.shard_map(
-        on_device,
+        functools.partial(chosen_plan, mesh),
         mesh=mesh,
         in_specs=placed,
         out_specs=(P(("dp", "grp")), P(("dp", "grp"), None), P(("dp", "grp"), None)),

time: 420 us -> 114 us (0.27)
  waiting for transfers between devices: 158 us -> 0 us
  local copies, waits for them, and re-layouts: 114 us -> 2.19 us
  Pallas kernels: 0 us -> 107 us
  starting transfers between devices: 75.3 us -> 0 us
  other arithmetic: 59 us -> 3.92 us
  matrix products: 10.6 us -> 0 us
    all_to_all x18 -> x0, waiting for transfers between devices: 158 us -> none  [the longest x1 69 us: route_grads(): lax.all_to_all(returned, 'dp', split_axis=2, concat_axis=2, tiled=True)]
    pallas_call x0 -> x5, Pallas kernels: none -> 107 us  [the longest x1 34.1 us: gather_rows(): pl.pallas_call(functools.partial(gather_kernel, depth), out_shape=jax.Sha...]
    all_to_all x18 -> x0, starting transfers between devices: 75.3 us -> none  [the longest x1 7.28 us: route_rows(): lax.all_to_all(col_tags, 'dp', split_axis=2, concat_axis=2, tiled=True)]
    gather x6 -> x0, local copies, waits for them, and re-layouts: 47.5 us -> none  [the longest x2 24.1 us: block_logits(): scores[row_iota, jnp.maximum(columns, 0)]]
    unnamed x6 -> x0, other arithmetic: 30.3 us -> none
    scatter x5 -> x0, local copies, waits for them, and re-layouts: 26.1 us -> none  [the longest x1 7.59 us: on_device(): jnp.zeros((slot_total,), jnp.bfloat16).at[places]]
    unnamed x44 -> x4, local copies, waits for them, and re-layouts: 19.2 us -> 2.19 us
    dot_general x3 -> x0, matrix products: 10.6 us -> none  [the longest x1 4.63 us: center_terms(): lax.dot_general(weights, scaled_rows, (((0,), (0,)), ((), ())), preferred...]
  transfers between devices with their start and end apart: 18 -> 0, of which waited for: 12 -> 0; matrix products, arithmetic and copies ran while one was open for 40% -> 0% of each run, Pallas kernels for 0% -> 0%
where the time goes in v1:
time: 114 us
  Pallas kernels  107 us (94%)
  other arithmetic  3.92 us (3%)
  local copies, waits for them, and re-layouts  2.19 us (2%)
    pallas_call x1, Pallas kernels, gather_rows(): pl.pallas_call(functools.partial(gather_kernel, depth), out_shape=jax.Sha...  34.1 us
    pallas_call x1, Pallas kernels, scatter_rows(): pl.pallas_call(functools.partial(scatter_kernel, depth), out_shape=jax.Sh...  32.2 us
    pallas_call x1, Pallas kernels, block_grads(): pl.pallas_call(functools.partial(grads_kernel, most), out_shape=(jax.Shap...  14 us
    pallas_call x1, Pallas kernels, block_scores(): pl.pallas_call(functools.partial(scores_kernel, most), out_shape=(jax.Sha...  13.3 us
    pallas_call x1, Pallas kernels, sample_totals(): pl.pallas_call(functools.partial(totals_kernel, depth), out_shape=(jax.Sh...  13.1 us

profile of v1, /device:TPU:0, one launch (start us, length us, event | category | flops | bytes accessed | tf_op | source)
XLA Modules:
  0.0 113.5 jit_solution(6152077704615549455)
XLA Ops:
  0.6 1.3 %fusion.12 = s32[]{:T(128)} fusion(s32[32]{0:T(128)} %param.10, s32[]{:T(128)S(6)} %add.12), kind=kLoop, calls=%fused_computation.21 | loop fusion | flops 95 | bytes 136 | tf_op jit(solution)/shard_map/reduce_sum | solution.py:852
  1.9 0.7 convert_bitcast_fusion.1
  2.6 0.7 convert_bitcast_fusion
  3.3 1.3 %fusion.8.tags_ref = bf16[16,512]{1,0:T(8,128)(2,1)} fusion(bf16[1,128]{1,0:T(2,128)(2,1)} %bitcast.9, bf16[1,128]{1,0:T(2,128)(2,1)S(1)} %get-tuple-element.26, bf16[1,128]{1,0:T(2,128)(2,1)S(1)} %get-tuple-element.25, bf16[8,128]{1,0:T(8,128)(2,1)S(1)} %convert_bitcast_fusion), kind=kLoop, calls=%fused_computation.10 | loop fusion | flops 155648 | bytes 19200 | tf_op jit(solution)/shard_map/concatenate | solution.py:854
  4.6 34.1 %gather_rows.1.g_ref = bf16[32,144,512]{2,1,0:T(8,128)(2,1)} custom-call(bf16[128,512]{1,0:T(8,128)(2,1)} %x_ref.3, bf16[16,512]{1,0:T(8,128)(2,1)} %fusion.8.tags_ref), custom_call_target="tpu_custom_call" | custom-call | tf_op jit(solution)/shard_map/gather_rows/pallas_call | solution.py:420
  38.7 13.3 %block_scores.1 = (bf16[1536,512]{1,0:T(8,128)(2,1)}, f32[1536,1024]{1,0:T(8,128)}, f32[32,128]{1,0:T(8,128)}, f32[32,128]{1,0:T(8,128)}, f32[32,128]{1,0:T(8,12...) custom-call(s32[1]{0:T(128)} %bitcast.block_ref, bf16[32,144,512]{2,1,0:T(8,128)(2,1)} %gather_rows.1.g_ref, bf16[1024,512]{1,0:T(8,128)(2,1)} %c_ref.3), custom_call_target="tpu_custom_call" | custom-call | tf_op jit(solution)/shard_map/block_scores/pallas_call | solution.py:511
  52.0 13.1 %sample_totals.1 = (f32[32,128]{1,0:T(8,128)}, f32[1,128]{1,0:T(1,128)}) custom-call(f32[32,128]{1,0:T(8,128)} %get-tuple-element.14.part_ref, f32[32,128]{1,0:T(8,128)} %get-tuple-element.15.pick_ref), custom_call_target="tpu_custom_call" | custom-call | tf_op jit(solution)/shard_map/sample_totals/pallas_call | solution.py:586
  65.1 0.0 copy-start
  65.1 14.0 %block_grads.1 = (bf16[32,128,512]{2,1,0:T(8,128)(2,1)}, bf16[1024,512]{1,0:T(8,128)(2,1)}) custom-call(f32[32,128]{1,0:T(8,128)} %get-tuple-element.17.total_ref, f32[32,128]{1,0:T(8,128)} %get-tuple-element.18.rank_ref, f32[32,128]{1,0:T(8,128)} %get-tuple-element.19.gain_ref, f32[1536,1]{1,0:T(8,128)} %get-tuple-element.20.colc_ref, ...), custom_call_target="tpu_custom_call" | custom-call | tf_op jit(solution)/shard_map/block_grads/pallas_call | solution.py:653
  79.1 32.2 %scatter_rows.1 = f32[128,512]{1,0:T(8,128)} custom-call(bf16[32,128,512]{2,1,0:T(8,128)(2,1)} %get-tuple-element.23.r_ref, bf16[128,512]{1,0:T(8,128)(2,1)} %x_ref.3), custom_call_target="tpu_custom_call" | custom-call | tf_op jit(solution)/shard_map/scatter_rows/pallas_call | solution.py:817
  111.3 0.0 copy-done
  111.3 0.5 copy.11
  111.9 1.7 %copy.12 = f32[128,512]{1,0:T(8,128)} copy(f32[128,512]{1,0:T(8,128)} %scatter_rows.1) | data formatting | bytes 524288
Async XLA Ops:
  65.1 46.2 %copy-start = (f32[1,128]{1,0:T(1,128)S(1)}, f32[1,128]{1,0:T(1,128)}, u32[]{:S(2)}) copy-start(f32[1,128]{1,0:T(1,128)} %get-tuple-element.16) | copy-start | bytes 1540

commit v2 on v0

--- a/solution.py
+++ b/solution.py
@@ -1,6 +1,10 @@
+import functools
+
 import jax
 import jax.numpy as jnp
 from jax import lax
+from jax.experimental import pallas as pl
+from jax.experimental.pallas import tpu as pltpu
 from jax.sharding import PartitionSpec as P
 
 BLOCK = 1024
@@ -253,6 +257,498 @@
     return (loss_out, feature_grad, grad_rows)
 
 
+MESH = pl.DeviceIdType.MESH
+VMEM = pl.BlockSpec(memory_space=pltpu.VMEM)
+TAG_ROWS = 16
+SPLIT = 32
+VMEM_LIMIT = 56 * 1024 * 1024
+
+
+class Place:
+    def __init__(self, depth):
+        dp, grp = lax.axis_index("dp"), lax.axis_index("grp")
+        self.depth = depth
+        self.z, y = lax.div(dp, 2), lax.rem(dp, 2)
+        x, self.c = lax.div(grp, 2), lax.rem(grp, 2)
+        self.a = y + self.c * (x - y)
+        self.b = x + self.c * (y - x)
+        self.me = dp * 4 + grp
+
+    def device(self, z, a, b, c):
+        y, x = a + c * (b - a), b + c * (a - b)
+        return (z * 2 + y, x * 2 + c)
+
+    def origin(self, z, a, b, c):
+        dp, grp = self.device(z, a, b, c)
+        return dp * 4 + grp
+
+    def up(self):
+        return self.device(self.z + 1, self.a, self.b, self.c)
+
+    def down(self):
+        return self.device(self.z - 1, self.a, self.b, self.c)
+
+    def first(self):
+        return self.device(self.z, 1 - self.a, self.b, self.c)
+
+    def second(self):
+        return self.device(self.z, self.a, 1 - self.b, self.c)
+
+    def sibling(self):
+        return self.device(self.z, self.b, self.a, 1 - self.c)
+
+    def inside(self, offset):
+        if offset == 0:
+            return None
+        return self.z + offset < self.depth if offset > 0 else self.z + offset >= 0
+
+    def when(self, offset, body):
+        if offset == 0:
+            body()
+        else:
+            pl.when(self.inside(offset))(body)
+
+
+def offsets_at(distance):
+    return [0] if distance == 0 else [-distance, distance]
+
+
+UP, DOWN, FIRST, SECOND, SIB = range(5)
+KINDS = 4
+
+
+def chosen(rank, most):
+    shape = (most, rank.shape[1])
+    return lax.broadcasted_iota(jnp.int32, shape, 0).astype(jnp.float32) == rank
+
+
+def one_hot(pick):
+    return jnp.where(pick, 1.0, 0.0).astype(jnp.bfloat16)
+
+
+def positives(columns, width):
+    shape = (columns.shape[0], width)
+    return lax.broadcasted_iota(jnp.int32, shape, 1).astype(jnp.float32) == columns
+
+
+def fused_kernel(
+    depth, most,
+    x_ref, scale_ref, blocks_ref, label_ref, slot_ref, c_ref,
+    loss_ref, out_ref, cg_ref,
+    g_ref, cn_ref, len_ref, xc_ref, e_ref, w_ref, rank_ref, gain_ref, colc_ref, held, landed,
+    r_ref, rs, tx2, rx2, tx1, rx1, txz, rxu, rxd,
+    send, recv, s_sum, v_sum, s_sib, v_sib, s2, v2, s1, v1, sz, vu, vd,
+):
+    f32, bf16 = jnp.float32, jnp.bfloat16
+    place = Place(depth)
+    z, a, b, c = place.z, place.a, place.b, place.c
+    rows, devices = x_ref.shape[0], g_ref.shape[0]
+    width = c_ref.shape[0]
+    turns = [place.device(lax.rem(z + k, depth), a, b, c) for k in range(1, depth)]
+    corner = place.device(z, 1 - a, 1 - b, c)
+    partners = [place.sibling(), place.first(), place.second(), corner] + turns
+    barrier = pltpu.get_barrier_semaphore()
+    for target in partners:
+        pl.semaphore_signal(barrier, inc=1, device_id=target, device_id_type=MESH)
+
+    widened = x_ref[...].astype(f32)
+    lengths = jnp.sqrt(jnp.sum(widened * widened, axis=1, keepdims=True) + EPSILON)
+    g_ref[place.me, 0:rows, :] = (widened / lengths).astype(bf16)
+    label = label_ref[...]
+    high = lax.div(label, SPLIT)
+    named = jnp.concatenate([blocks_ref[...].astype(f32), jnp.zeros((rows, rows - 8), f32)], axis=1)
+    tags = jnp.concatenate(
+        [
+            jnp.transpose(named)[0:8],
+            high.astype(f32),
+            (label - high * SPLIT).astype(f32),
+            scale_ref[...].astype(f32),
+            jnp.zeros((TAG_ROWS - 11, rows), f32),
+        ],
+        axis=0,
+    )
+    g_ref[place.me, rows : rows + TAG_ROWS, :] = jnp.zeros((TAG_ROWS, x_ref.shape[1]), bf16)
+    g_ref[place.me, rows : rows + TAG_ROWS, 0:rows] = tags.astype(bf16)
+    slots = slot_ref[...]
+    mine = jnp.sum(
+        jnp.where(slots == place.me, lax.broadcasted_iota(jnp.int32, slots.shape, 1), 0).astype(f32),
+        axis=1,
+        keepdims=True,
+    )
+    pl.semaphore_wait(barrier, len(partners))
+
+    def copy(src, dst, send_sem, recv_sem, target):
+        return pltpu.make_async_remote_copy(
+            src_ref=src, dst_ref=dst, send_sem=send_sem, recv_sem=recv_sem, device_id=target, device_id_type=MESH
+        )
+
+    def package(slot, way, target):
+        return copy(g_ref.at[slot], g_ref.at[slot], send.at[way, slot], recv.at[slot], target)
+
+    def arrived(slot):
+        package(slot, SIB, place.sibling()).wait_recv()
+
+    def origin(cls, kind, level):
+        if cls == 0:
+            return place.origin(level, 1 - a if kind & 1 else a, 1 - b if kind & 2 else b, c)
+        return place.origin(level, 1 - b if kind & 1 else b, 1 - a if kind & 2 else a, 1 - c)
+
+    def handle(off, kind, act, wait):
+        def body():
+            slot = origin(0, kind, z + off)
+            if wait and (off != 0 or kind != 0):
+                arrived(slot)
+            if kind == 0 and off <= 0:
+                pl.when(z < depth - 1)(lambda: act(package(slot, UP, place.up())))
+            if kind == 0 and off >= 0:
+                pl.when(z > 0)(lambda: act(package(slot, DOWN, place.down())))
+            if kind < 2:
+                act(package(slot, SECOND, place.second()))
+            if kind < 1:
+                act(package(slot, FIRST, place.first()))
+            act(package(slot, SIB, place.sibling()))
+
+        place.when(off, body)
+
+    def events(r):
+        if r < depth:
+            for off in offsets_at(r):
+                yield off, 0
+        if 1 <= r <= depth:
+            for off in offsets_at(r - 1):
+                yield off, 1
+                yield off, 2
+        if 2 <= r <= depth + 1:
+            for off in offsets_at(r - 2):
+                yield off, 3
+
+    def span(j, level=None):
+        if level is None:
+            return slice(j * depth * most, (j + 1) * depth * most)
+        return slice((j * depth + level) * most, (j * depth + level + 1) * most)
+
+    def stacked(parts):
+        return jnp.concatenate(parts, axis=0)
+
+    def score(cls, kind):
+        j = cls * KINDS + kind
+        levels = range(depth)
+        where_from = [origin(cls, kind, level) for level in levels]
+        if cls == 1:
+            for o in where_from:
+                arrived(o)
+        tagged = [g_ref[o, rows : rows + TAG_ROWS, 0:rows].astype(f32) for o in where_from]
+        hits = [jnp.where(t[0:8] == mine, 1.0, 0.0) for t in tagged]
+        wanted = stacked([jnp.sum(hit, axis=0, keepdims=True) for hit in hits])
+        shape = (rows, rows)
+        earlier = lax.broadcasted_iota(jnp.int32, shape, 0) < lax.broadcasted_iota(jnp.int32, shape, 1)
+        padded = stacked([wanted, jnp.zeros((16 - depth % 16, rows), f32)]).astype(bf16)
+        ahead = jnp.dot(padded, one_hot(earlier), preferred_element_type=f32)[0:depth]
+        rank = jnp.where(wanted > 0.0, ahead, -1.0)
+        picks, columns = [], []
+        for level in levels:
+            p = j * depth + level
+            rank_ref[p : p + 1, :] = rank[level : level + 1]
+            gain_ref[p : p + 1, :] = tagged[level][10:11]
+            pick = chosen(rank[level : level + 1], most)
+            column = jnp.where(hits[level][0:1] > 0.0, tagged[level][8:9] * SPLIT + tagged[level][9:10] + 1.0, 0.0)
+            picks.append(pick)
+            columns.append(jnp.sum(jnp.where(pick, column, 0.0), axis=1, keepdims=True) - 1.0)
+            xc_ref[span(j, level), :] = jnp.dot(
+                one_hot(pick), g_ref[where_from[level], 0:rows, :], preferred_element_type=f32
+            ).astype(bf16)
+        columns = stacked(columns)
+        colc_ref[span(j), :] = columns
+        scores = lax.dot_general(
+            xc_ref[span(j), :], cn_ref[...], (((1,), (1,)), ((), ())), preferred_element_type=f32
+        )
+        positive = positives(columns, width)
+        scores = scores - jnp.where(positive, LOGIT_SCALE * MARGIN, 0.0)
+        exps = jnp.exp(scores)
+        e_ref[span(j), :] = exps
+        sums = jnp.sum(exps, axis=1, keepdims=True)
+        target = jnp.sum(jnp.where(positive, scores, 0.0), axis=1, keepdims=True)
+        for level in levels:
+            at = slice(level * most, (level + 1) * most)
+            o = where_from[level]
+            held[0, pl.ds(o, 1), :] = jnp.sum(jnp.where(picks[level], sums[at], 0.0), axis=0, keepdims=True)
+            held[0, pl.ds(o + devices, 1), :] = jnp.sum(
+                jnp.where(picks[level], target[at], 0.0), axis=0, keepdims=True
+            )
+
+    start = lambda item: item.start()
+    for r in range(depth + 2):
+        for off, kind in events(r):
+            handle(off, kind, start, True)
+        if r == 0:
+            centers = c_ref[...].astype(f32)
+            center_len = jnp.sqrt(jnp.sum(centers * centers, axis=1, keepdims=True) + EPSILON)
+            len_ref[...] = center_len
+            cn_ref[...] = ((centers / center_len).astype(bf16) * LOGIT_SCALE).astype(bf16)
+        if r == depth - 1:
+            score(0, 0)
+            score(1, 0)
+        if r == depth:
+            score(0, 1)
+    for cls, kind in ((1, 1), (0, 2), (1, 2), (0, 3), (1, 3)):
+        score(cls, kind)
+
+    started = []
+
+    def share(n, src, target):
+        item = copy(held.at[src], landed.at[n], s_sum.at[n], v_sum.at[n], target)
+        item.start()
+        started.append(item)
+
+    share(0, 0, partners[0])
+    started[0].wait_recv()
+    held[1] = held[0] + landed[0]
+    for n in (1, 2, 3):
+        share(n, 1, partners[n])
+    for n in (1, 2, 3):
+        started[n].wait_recv()
+    held[2] = (held[1] + landed[1]) + (landed[2] + landed[3])
+    for n in range(4, len(partners)):
+        share(n, 2, partners[n])
+    for n in range(4, len(partners)):
+        started[n].wait_recv()
+    total = held[2]
+    for n in range(4, len(partners)):
+        total = total + landed[n]
+    held[3] = total
+
+    def grads(cls, kind):
+        j = cls * KINDS + kind
+        picks, factors, gains = [], [], []
+        for level in range(depth):
+            p = j * depth + level
+            pick = chosen(rank_ref[p : p + 1, :], most)
+            gain = gain_ref[p : p + 1, :]
+            factor = gain / held[3, pl.ds(origin(cls, kind, level), 1), :]
+            picks.append(pick)
+            factors.append(jnp.sum(jnp.where(pick, factor, 0.0), axis=1, keepdims=True))
+            gains.append(jnp.sum(jnp.where(pick, gain, 0.0), axis=1, keepdims=True))
+        positive = positives(colc_ref[span(j), :], width)
+        weights = e_ref[span(j), :] * stacked(factors) - jnp.where(positive, stacked(gains), 0.0)
+        weights = weights.astype(bf16)
+        w_ref[span(j), :] = weights
+        returned = jnp.dot(weights, cn_ref[...], preferred_element_type=f32).astype(bf16)
+        for level in range(depth):
+            r_ref[j * depth + level] = lax.dot_general(
+                one_hot(picks[level]),
+                returned[level * most : (level + 1) * most],
+                (((0,), (0,)), ((), ())),
+                preferred_element_type=f32,
+            ).astype(bf16)
+
+    def center_rows(n, pieces):
+        size = width // pieces
+        at = slice(n * size, (n + 1) * size)
+        grad = LOGIT_SCALE * lax.dot_general(
+            w_ref[:, at], xc_ref[...], (((0,), (0,)), ((), ())), preferred_element_type=f32
+        )
+        lens = len_ref[at, :]
+        unit = c_ref[at, :].astype(f32) / lens
+        along = jnp.sum(unit * grad, axis=1, keepdims=True)
+        cg_ref[at, :] = ((grad - unit * along) / lens).astype(bf16)
+
+    def to_sibling(kind, level):
+        slot = kind * depth + level
+        return copy(
+            r_ref.at[(KINDS + kind) * depth + level], rs.at[slot], s_sib.at[slot], v_sib.at[slot], place.sibling()
+        )
+
+    def to_second(kind, level):
+        slot = (kind & 1) * depth + level
+        return copy(tx2.at[slot], rx2.at[slot], s2.at[slot], v2.at[slot], place.second())
+
+    def to_first(level):
+        return copy(tx1.at[level], rx1.at[level], s1.at[level], v1.at[level], place.first())
+
+    def to_up(slot):
+        return copy(txz.at[slot], rxu.at[slot], sz.at[slot], vu.at[slot], place.up())
+
+    def to_down(slot):
+        return copy(txz.at[slot], rxd.at[slot], sz.at[slot], vd.at[slot], place.down())
+
+    def own_sum(kind, level):
+        to_sibling(kind, level).wait_recv()
+        slot = kind * depth + level
+        return r_ref[slot].astype(f32) + rs[slot].astype(f32)
+
+    for kind in (3, 2):
+        grads(1, kind)
+        for level in range(depth):
+            to_sibling(kind, level).start()
+        grads(0, kind)
+        for level in range(depth):
+            tx2[(kind & 1) * depth + level] = own_sum(kind, level).astype(bf16)
+            to_second(kind, level).start()
+    for kind in (1, 0):
+        grads(1, kind)
+        for level in range(depth):
+            to_sibling(kind, level).start()
+    grads(0, 1)
+    grads(0, 0)
+    center_rows(0, 4)
+    for level in range(depth):
+        total = own_sum(1, level)
+        to_second(3, level).wait_recv()
+        tx1[level] = (total + rx2[depth + level].astype(f32)).astype(bf16)
+        to_first(level).start()
+    center_rows(1, 4)
+
+    def gathered_sum(level):
+        total = rs[level].astype(f32) + r_ref[level].astype(f32)
+        return total + rx2[level].astype(f32) + rx1[level].astype(f32)
+
+    for level in range(depth):
+        to_sibling(0, level).wait_recv()
+        to_second(2, level).wait_recv()
+        to_first(level).wait_recv()
+
+    for r in range(depth - 1, 0, -1):
+        for off in offsets_at(r):
+
+            def cross_z():
+                slot = z + off
+                item = to_up(slot) if off > 0 else to_down(slot)
+                txz[slot] = gathered_sum(slot).astype(bf16)
+
+                @pl.when(z > 0 if off > 0 else z < depth - 1)
+                def _():
+                    item.wait_recv()
+                    arriving = rxu if off > 0 else rxd
+                    txz[slot] = (txz[slot].astype(f32) + arriving[slot].astype(f32)).astype(bf16)
+
+                item.start()
+
+            place.when(off, cross_z)
+    center_rows(2, 4)
+    center_rows(3, 4)
+
+    out_ref[...] = gathered_sum(z)
+
+    @pl.when(z > 0)
+    def _():
+        to_up(z).wait_recv()
+        out_ref[...] += rxu[z].astype(f32)
+
+    @pl.when(z < depth - 1)
+    def _():
+        to_down(z).wait_recv()
+        out_ref[...] += rxd[z].astype(f32)
+
+    widened = x_ref[...].astype(f32)
+    lengths = jnp.sqrt(jnp.sum(widened * widened, axis=1, keepdims=True) + EPSILON)
+    unit = widened / lengths
+    grad = out_ref[...]
+    along = jnp.sum(unit * grad, axis=1, keepdims=True)
+    out_ref[...] = (grad - unit * along) / lengths
+    loss_ref[...] = jnp.log(held[3, pl.ds(place.me, 1), :]) - held[3, pl.ds(place.me + devices, 1), :]
+
+    for r in range(depth + 2):
+        for off, kind in events(r):
+            handle(off, kind, lambda item: item.wait_send(), False)
+    for item in started:
+        item.wait_send()
+    for level in range(depth):
+        for kind in range(KINDS):
+            to_sibling(kind, level).wait_send()
+        for kind in (3, 2):
+            to_second(kind, level).wait_send()
+        to_first(level).wait_send()
+    for r in range(1, depth):
+        for off in offsets_at(r):
+            place.when(off, lambda: (to_up if off > 0 else to_down)(z + off).wait_send())
+
+
+def on_device_dense(depth, most, features, loss_scale, blocks, label_col, block_slot, centers):
+    devices = depth * 8
+    rows, width = features.shape
+    capacity = devices * most
+    f32, bf16 = jnp.float32, jnp.bfloat16
+
+    def slots(count):
+        return pltpu.VMEM((count, rows, width), bf16)
+
+    def sems(*shape):
+        return pltpu.SemaphoreType.DMA(shape)
+
+    loss, feature_grad, center_grad = pl.pallas_call(
+        functools.partial(fused_kernel, depth, most),
+        out_shape=(
+            jax.ShapeDtypeStruct((1, rows), f32),
+            jax.ShapeDtypeStruct((rows, width), f32),
+            jax.ShapeDtypeStruct(centers.shape, bf16),
+        ),
+        in_specs=[VMEM] * 6,
+        out_specs=(VMEM,) * 3,
+        scratch_shapes=[
+            pltpu.VMEM((devices, rows + TAG_ROWS, width), bf16),
+            pltpu.VMEM(centers.shape, bf16),
+            pltpu.VMEM((centers.shape[0], 1), f32),
+            pltpu.VMEM((capacity, width), bf16),
+            pltpu.VMEM((capacity, centers.shape[0]), f32),
+            pltpu.VMEM((capacity, centers.shape[0]), bf16),
+            pltpu.VMEM((devices, rows), f32),
+            pltpu.VMEM((devices, rows), f32),
+            pltpu.VMEM((capacity, 1), f32),
+            pltpu.VMEM((4, 2 * devices, rows), f32),
+            pltpu.VMEM((depth + 3, 2 * devices, rows), f32),
+            slots(devices),
+            slots(devices // 2),
+            slots(depth * 2),
+            slots(depth * 2),
+            slots(depth),
+            slots(depth),
+            slots(depth),
+            slots(depth),
+            slots(depth),
+            sems(5, devices),
+            sems(devices),
+            sems(depth + 3),
+            sems(depth + 3),
+            sems(devices // 2),
+            sems(devices // 2),
+            sems(depth * 2),
+            sems(depth * 2),
+            sems(depth),
+            sems(depth),
+            sems(depth),
+            sems(depth),
+            sems(depth),
+        ],
+        compiler_params=pltpu.CompilerParams(
+            collective_id=0, has_side_effects=True, vmem_limit_bytes=VMEM_LIMIT
+        ),
+        name="partial_softmax",
+    )(features, loss_scale[None], blocks, label_col[None], block_slot[None], centers)
+    return loss.reshape(-1), feature_grad, center_grad
+
+
+def chosen_plan(mesh, features, loss_scale, blocks, label_col, block_slot, centers):
+    dp_count, groups = mesh.shape["dp"], mesh.shape["grp"]
+    rows, picks = blocks.shape
+    total = block_slot.shape[0]
+    quota = (rows * picks + total - 1) // total
+    most = quota + max(1, quota // 2)
+    dense = (
+        most * 4 >= rows
+        and most % 16 == 0
+        and rows == 128
+        and groups == 4
+        and dp_count % 2 == 0
+        and total == dp_count * groups
+        and total <= 256
+        and picks == 8
+    )
+    args = (features, loss_scale, blocks, label_col, block_slot, centers)
+    if dense:
+        return on_device_dense(dp_count // 2, most, *args)
+    return on_device(*args)
+
+
 def solution(mesh):
     placed = (
         P(("dp", "grp"), None),
@@ -263,7 +759,7 @@
         P(("dp", "grp"), None),
     )
     return jax.shard_map(
-        on_device,
+        functools.partial(chosen_plan, mesh),
         mesh=mesh,
         in_specs=placed,
         out_specs=(P(("dp", "grp")), P(("dp", "grp"), None), P(("dp", "grp"), None)),

time: 420 us -> 88.4 us (0.21)
  waiting for transfers between devices: 158 us -> 0 us
  local copies, waits for them, and re-layouts: 114 us -> 6.45 us
  Pallas kernels: 0 us -> 81 us
  starting transfers between devices: 75.3 us -> 0 us
  other arithmetic: 59 us -> 0 us
  matrix products: 10.6 us -> 0 us
    all_to_all x18 -> x0, waiting for transfers between devices: 158 us -> none  [the longest x1 69 us: route_grads(): lax.all_to_all(returned, 'dp', split_axis=2, concat_axis=2, tiled=True)]
    pallas_call x0 -> x1, Pallas kernels: none -> 81 us  [on_device_dense(): pl.pallas_call(functools.partial(fused_kernel, depth, most), out_shape=(j...]
    all_to_all x18 -> x0, starting transfers between devices: 75.3 us -> none  [the longest x1 7.28 us: route_rows(): lax.all_to_all(col_tags, 'dp', split_axis=2, concat_axis=2, tiled=True)]
    gather x6 -> x0, local copies, waits for them, and re-layouts: 47.5 us -> none  [the longest x2 24.1 us: block_logits(): scores[row_iota, jnp.maximum(columns, 0)]]
    unnamed x6 -> x0, other arithmetic: 30.3 us -> none
    scatter x5 -> x0, local copies, waits for them, and re-layouts: 26.1 us -> none  [the longest x1 7.59 us: on_device(): jnp.zeros((slot_total,), jnp.bfloat16).at[places]]
    unnamed x44 -> x8, local copies, waits for them, and re-layouts: 19.2 us -> 6.45 us
    dot_general x3 -> x0, matrix products: 10.6 us -> none  [the longest x1 4.63 us: center_terms(): lax.dot_general(weights, scaled_rows, (((0,), (0,)), ((), ())), preferred...]
  transfers between devices with their start and end apart: 18 -> 0, of which waited for: 12 -> 0; matrix products, arithmetic and copies ran while one was open for 40% -> 0% of each run, Pallas kernels for 0% -> 0%
where the time goes in v2:
time: 88.4 us; the launch traced here: 88.1 us
  Pallas kernels  81 us (92%)
  local copies, waits for them, and re-layouts  6.45 us (7%)
    pallas_call x1, Pallas kernels, on_device_dense(): pl.pallas_call(functools.partial(fused_kernel, depth, most), out_shape=(j...  81 us
    unnamed x8, local copies, waits for them, and re-layouts  6.45 us

profile of v2, /device:TPU:0, one launch (start us, length us, event | category | flops | bytes accessed | tf_op | source)
XLA Modules:
  0.0 88.1 jit_solution(2861315568419642748)
XLA Ops:
  0.6 0.0 copy-start
  0.6 0.7 copy-done
  1.3 0.7 copy.9.blocks_ref
  2.0 81.0 %partial_softmax.1 = (f32[1,128]{1,0:T(1,128)}, f32[128,512]{1,0:T(8,128)}, bf16[1024,512]{1,0:T(8,128)(2,1)}) custom-call(bf16[128,512]{1,0:T(8,128)(2,1)} %x_ref.1, bf16[1,128]{1,0:T(2,128)(2,1)} %bitcast.4, s32[128,8]{1,0:T(8,128)} %copy.9.blocks_ref, s32[1,128]{1,0:T(1,128)} %bitcast.5, s32[1,32]{1,0:T(1,128)} %bitcast.6, bf16[1024,512]{1,0:T(8,128)(2,1)} %c_ref.1), custom_call_target="tpu_custom_call" | custom-call | tf_op jit(solution)/shard_map/partial_softmax/pallas_call | solution.py:678
  83.1 0.0 copy-start.1
  83.1 0.6 copy-done.1
  83.7 0.5 copy.13
  84.2 1.7 %copy.14 = f32[128,512]{1,0:T(8,128)} copy(f32[128,512]{1,0:T(8,128)} %get-tuple-element.13) | data formatting | bytes 524288
  85.9 2.3 %copy.15 = bf16[1024,512]{1,0:T(8,128)(2,1)} copy(bf16[1024,512]{1,0:T(8,128)(2,1)} %get-tuple-element.14) | data formatting | bytes 2097152
Async XLA Ops:
  0.6 0.7 copy-start
  83.1 0.6 copy-start.1

commit v3 on v2

--- a/solution.py
+++ b/solution.py
@@ -335,7 +335,7 @@
     depth, most,
     x_ref, scale_ref, blocks_ref, label_ref, slot_ref, c_ref,
     loss_ref, out_ref, cg_ref,
-    g_ref, cn_ref, len_ref, xc_ref, e_ref, w_ref, rank_ref, gain_ref, colc_ref, held, landed,
+    g_ref, cn_ref, cnt_ref, len_ref, xc_ref, e_ref, w_ref, rank_ref, gain_ref, colc_ref, held, landed,
     r_ref, rs, tx2, rx2, tx1, rx1, txz, rxu, rxd,
     send, recv, s_sum, v_sum, s_sib, v_sib, s2, v2, s1, v1, sz, vu, vd,
 ):
@@ -460,7 +460,7 @@
         columns = stacked(columns)
         colc_ref[span(j), :] = columns
         scores = lax.dot_general(
-            xc_ref[span(j), :], cn_ref[...], (((1,), (1,)), ((), ())), preferred_element_type=f32
+            xc_ref[span(j), :], cnt_ref[...], (((1,), (0,)), ((), ())), preferred_element_type=f32
         )
         positive = positives(columns, width)
         scores = scores - jnp.where(positive, LOGIT_SCALE * MARGIN, 0.0)
@@ -477,21 +477,33 @@
             )
 
     start = lambda item: item.start()
-    for r in range(depth + 2):
-        for off, kind in events(r):
-            handle(off, kind, start, True)
-        if r == 0:
-            centers = c_ref[...].astype(f32)
-            center_len = jnp.sqrt(jnp.sum(centers * centers, axis=1, keepdims=True) + EPSILON)
-            len_ref[...] = center_len
-            cn_ref[...] = ((centers / center_len).astype(bf16) * LOGIT_SCALE).astype(bf16)
-        if r == depth - 1:
-            score(0, 0)
-            score(1, 0)
-        if r == depth:
-            score(0, 1)
-    for cls, kind in ((1, 1), (0, 2), (1, 2), (0, 3), (1, 3)):
-        score(cls, kind)
+
+    def pass_on(kind, distances):
+        for r in distances:
+            for off in offsets_at(r):
+                handle(off, kind, start, True)
+
+    pass_on(0, [0])
+    centers = c_ref[...].astype(f32)
+    center_len = jnp.sqrt(jnp.sum(centers * centers, axis=1, keepdims=True) + EPSILON)
+    len_ref[...] = center_len
+    cn_ref[...] = ((centers / center_len).astype(bf16) * LOGIT_SCALE).astype(bf16)
+    cnt_ref[...] = jnp.transpose(cn_ref[...])
+    for r in range(1, depth):
+        pass_on(0, [r])
+        pass_on(1, [r - 1])
+    score(0, 0)
+    pass_on(1, [depth - 1])
+    score(1, 0)
+    pass_on(2, range(depth))
+    score(0, 1)
+    score(1, 1)
+    pass_on(3, range(depth - 1))
+    score(0, 2)
+    score(1, 2)
+    pass_on(3, [depth - 1])
+    score(0, 3)
+    score(1, 3)
 
     started = []
 
@@ -576,36 +588,36 @@
         slot = kind * depth + level
         return r_ref[slot].astype(f32) + rs[slot].astype(f32)
 
+    upper = lax.div(2 * z, depth)
+    far_first = [upper * k + (1 - upper) * (depth - 1 - k) for k in range(depth)]
+
+    def give_sibling(kind):
+        grads(1, kind)
+        for level in far_first:
+            to_sibling(kind, level).start()
+
     for kind in (3, 2):
-        grads(1, kind)
-        for level in range(depth):
-            to_sibling(kind, level).start()
+        give_sibling(kind)
         grads(0, kind)
-        for level in range(depth):
+        for level in far_first:
             tx2[(kind & 1) * depth + level] = own_sum(kind, level).astype(bf16)
             to_second(kind, level).start()
-    for kind in (1, 0):
-        grads(1, kind)
-        for level in range(depth):
-            to_sibling(kind, level).start()
+    give_sibling(1)
     grads(0, 1)
-    grads(0, 0)
-    center_rows(0, 4)
-    for level in range(depth):
+    for level in far_first:
         total = own_sum(1, level)
         to_second(3, level).wait_recv()
         tx1[level] = (total + rx2[depth + level].astype(f32)).astype(bf16)
         to_first(level).start()
-    center_rows(1, 4)
+    give_sibling(0)
+    grads(0, 0)
+    center_rows(0, 4)
 
     def gathered_sum(level):
-        total = rs[level].astype(f32) + r_ref[level].astype(f32)
-        return total + rx2[level].astype(f32) + rx1[level].astype(f32)
-
-    for level in range(depth):
-        to_sibling(0, level).wait_recv()
+        total = own_sum(0, level)
         to_second(2, level).wait_recv()
         to_first(level).wait_recv()
+        return total + rx2[level].astype(f32) + rx1[level].astype(f32)
 
     for r in range(depth - 1, 0, -1):
         for off in offsets_at(r):
@@ -624,8 +636,8 @@
                 item.start()
 
             place.when(off, cross_z)
-    center_rows(2, 4)
-    center_rows(3, 4)
+    for n in (1, 2, 3):
+        center_rows(n, 4)
 
     out_ref[...] = gathered_sum(z)
 
@@ -687,6 +699,7 @@
         scratch_shapes=[
             pltpu.VMEM((devices, rows + TAG_ROWS, width), bf16),
             pltpu.VMEM(centers.shape, bf16),
+            pltpu.VMEM(centers.shape[::-1], bf16),
             pltpu.VMEM((centers.shape[0], 1), f32),
             pltpu.VMEM((capacity, width), bf16),
             pltpu.VMEM((capacity, centers.shape[0]), f32),

time: 88.4 us -> 79.4 us (0.90)
  Pallas kernels: 81 us -> 72 us
    pallas_call x1, Pallas kernels: 81 us -> 72 us  [on_device_dense(): pl.pallas_call(functools.partial(fused_kernel, depth, most), out_shape=(j...]
where the time goes in v3:
time: 79.4 us; the launch traced here: 79.2 us
  Pallas kernels  72 us (91%)
  local copies, waits for them, and re-layouts  6.45 us (8%)
    pallas_call x1, Pallas kernels, on_device_dense(): pl.pallas_call(functools.partial(fused_kernel, depth, most), out_shape=(j...  72 us
    unnamed x8, local copies, waits for them, and re-layouts  6.45 us

profile of v3, /device:TPU:0, one launch (start us, length us, event | category | flops | bytes accessed | tf_op | source)
XLA Modules:
  0.0 79.2 jit_solution(4189457092047251216)
XLA Ops:
  0.6 0.0 copy-start
  0.6 0.7 copy-done
  1.3 0.7 copy.9.blocks_ref
  2.0 72.0 %partial_softmax.1 = (f32[1,128]{1,0:T(1,128)}, f32[128,512]{1,0:T(8,128)}, bf16[1024,512]{1,0:T(8,128)(2,1)}) custom-call(bf16[128,512]{1,0:T(8,128)(2,1)} %x_ref.1, bf16[1,128]{1,0:T(2,128)(2,1)} %bitcast.4, s32[128,8]{1,0:T(8,128)} %copy.9.blocks_ref, s32[1,128]{1,0:T(1,128)} %bitcast.5, s32[1,32]{1,0:T(1,128)} %bitcast.6, bf16[1024,512]{1,0:T(8,128)(2,1)} %c_ref.1), custom_call_target="tpu_custom_call" | custom-call | tf_op jit(solution)/shard_map/partial_softmax/pallas_call | solution.py:690
  74.1 0.0 copy-start.1
  74.1 0.6 copy-done.1
  74.7 0.5 copy.13
  75.2 1.7 %copy.14 = f32[128,512]{1,0:T(8,128)} copy(f32[128,512]{1,0:T(8,128)} %get-tuple-element.13) | data formatting | bytes 524288
  76.9 2.3 %copy.15 = bf16[1024,512]{1,0:T(8,128)(2,1)} copy(bf16[1024,512]{1,0:T(8,128)(2,1)} %get-tuple-element.14) | data formatting | bytes 2097152
Async XLA Ops:
  0.6 0.7 copy-start
  74.1 0.6 copy-start.1

commit v4 on v3

--- a/solution.py
+++ b/solution.py
@@ -356,10 +356,9 @@
     g_ref[place.me, 0:rows, :] = (widened / lengths).astype(bf16)
     label = label_ref[...]
     high = lax.div(label, SPLIT)
-    named = jnp.concatenate([blocks_ref[...].astype(f32), jnp.zeros((rows, rows - 8), f32)], axis=1)
     tags = jnp.concatenate(
         [
-            jnp.transpose(named)[0:8],
+            blocks_ref[...].astype(f32),
             high.astype(f32),
             (label - high * SPLIT).astype(f32),
             scale_ref[...].astype(f32),
@@ -651,12 +650,6 @@
         to_down(z).wait_recv()
         out_ref[...] += rxd[z].astype(f32)
 
-    widened = x_ref[...].astype(f32)
-    lengths = jnp.sqrt(jnp.sum(widened * widened, axis=1, keepdims=True) + EPSILON)
-    unit = widened / lengths
-    grad = out_ref[...]
-    along = jnp.sum(unit * grad, axis=1, keepdims=True)
-    out_ref[...] = (grad - unit * along) / lengths
     loss_ref[...] = jnp.log(held[3, pl.ds(place.me, 1), :]) - held[3, pl.ds(place.me + devices, 1), :]
 
     for r in range(depth + 2):
@@ -675,6 +668,28 @@
             place.when(off, lambda: (to_up if off > 0 else to_down)(z + off).wait_send())
 
 
+def finish_kernel(loss_ref, grad_ref, cg_ref, x_ref, loss_out, out_ref, cg_out):
+    loss_out[...] = loss_ref[...]
+    cg_out[...] = cg_ref[...]
+    widened = x_ref[...].astype(jnp.float32)
+    lengths = jnp.sqrt(jnp.sum(widened * widened, axis=1, keepdims=True) + EPSILON)
+    unit = widened / lengths
+    grad = grad_ref[...]
+    along = jnp.sum(unit * grad, axis=1, keepdims=True)
+    out_ref[...] = (grad - unit * along) / lengths
+
+
+def finish(loss, unit_grad, center_grad, features):
+    loss, feature_grad, center_grad = pl.pallas_call(
+        finish_kernel,
+        out_shape=tuple(jax.ShapeDtypeStruct(part.shape, part.dtype) for part in (loss, unit_grad, center_grad)),
+        in_specs=[VMEM] * 4,
+        out_specs=(VMEM,) * 3,
+        name="finish",
+    )(loss, unit_grad, center_grad, features)
+    return loss.reshape(-1), feature_grad, center_grad
+
+
 def on_device_dense(depth, most, features, loss_scale, blocks, label_col, block_slot, centers):
     devices = depth * 8
     rows, width = features.shape
@@ -687,7 +702,7 @@
     def sems(*shape):
         return pltpu.SemaphoreType.DMA(shape)
 
-    loss, feature_grad, center_grad = pl.pallas_call(
+    loss, unit_grad, center_grad = pl.pallas_call(
         functools.partial(fused_kernel, depth, most),
         out_shape=(
             jax.ShapeDtypeStruct((1, rows), f32),
@@ -736,8 +751,8 @@
             collective_id=0, has_side_effects=True, vmem_limit_bytes=VMEM_LIMIT
         ),
         name="partial_softmax",
-    )(features, loss_scale[None], blocks, label_col[None], block_slot[None], centers)
-    return loss.reshape(-1), feature_grad, center_grad
+    )(features, loss_scale[None], blocks.T, label_col[None], block_slot[None], centers)
+    return finish(loss, unit_grad, center_grad, features)
 
 
 def chosen_plan(mesh, features, loss_scale, blocks, label_col, block_slot, centers):

time: 79.4 us -> 75.2 us (0.947)
  local copies, waits for them, and re-layouts: 6.45 us -> 0 us
  Pallas kernels: 72 us -> 74.4 us
    unnamed x8 -> x0, local copies, waits for them, and re-layouts: 6.45 us -> none
    pallas_call x0 -> x1, Pallas kernels: none -> 2.61 us  [finish(): pl.pallas_call(finish_kernel, out_shape=tuple((jax.ShapeDtypeStruct(part....]
where the time goes in v4:
time: 75.2 us; the launch traced here: 75 us
  Pallas kernels  74.4 us (99%)
    pallas_call x1, Pallas kernels, on_device_dense(): pl.pallas_call(functools.partial(fused_kernel, depth, most), out_shape=(j...  71.8 us
    pallas_call x1, Pallas kernels, finish(): pl.pallas_call(finish_kernel, out_shape=tuple((jax.ShapeDtypeStruct(part....  2.61 us

profile of v4, /device:TPU:0, one launch (start us, length us, event | category | flops | bytes accessed | tf_op | source)
XLA Modules:
  0.0 75.0 jit_solution(11439245280927001084)
XLA Ops:
  0.6 71.8 %partial_softmax.1 = (f32[1,128]{1,0:T(1,128)}, f32[128,512]{1,0:T(8,128)}, bf16[1024,512]{1,0:T(8,128)(2,1)}) custom-call(bf16[128,512]{1,0:T(8,128)(2,1)} %x_ref.3, bf16[1,128]{1,0:T(2,128)(2,1)} %bitcast.6, s32[8,128]{1,0:T(8,128)} %bitcast.5, s32[1,128]{1,0:T(1,128)} %bitcast.7, s32[1,32]{1,0:T(1,128)} %bitcast.8, bf16[1024,512]{1,0:T(8,128)(2,1)} %c_ref.1), custom_call_target="tpu_custom_call" | custom-call | tf_op jit(solution)/shard_map/partial_softmax/pallas_call | solution.py:705
  72.4 2.6 %finish.1 = (f32[1,128]{1,0:T(1,128)}, f32[128,512]{1,0:T(8,128)}, bf16[1024,512]{1,0:T(8,128)(2,1)}) custom-call(f32[1,128]{1,0:T(1,128)} %get-tuple-element.9.loss_ref, f32[128,512]{1,0:T(8,128)} %get-tuple-element.10.grad_ref, bf16[1024,512]{1,0:T(8,128)(2,1)} %get-tuple-element.11.cg_ref, bf16[128,512]{1,0:T(8,128)(2,1)} %x_ref.3), custom_call_target="tpu_custom_call" | custom-call | tf_op jit(solution)/shard_map/finish/pallas_call | solution.py:683
